TPU v7x, 512 devices: a whole 4x8x8 slice. The times are simulated.
512 devices in a mesh: gy: 16 (over y, core), gx: 32 (over z, x).
Axes of the slice: x: 4, y: 8, z: 8, core: 2. Of those that a mesh axis runs over, the one named last changes fastest.
Arguments:
- pressure: float32 [512, 256, 128], P('gx', 'gy'), may hold values from -0.03 to 0.03
- source: float32 [512, 256, 128], P('gx', 'gy'), may hold values from -0.2 to 0.2
- porosity: bfloat16 [512, 256, 128], P('gx', 'gy'), may hold values from 0.079589844 to 0.34960938
- permeability: bfloat16 [512, 256, 128], P('gx', 'gy'), may hold values from 0.25 to 4
- speed: bfloat16 [512, 256, 128], P('gx', 'gy'), may hold values from 0.099609375 to 3
Outputs:
- updated: float32 [512, 256, 128], P('gx', 'gy')
All inputs are finite; a program needn't handle non-finite values.
Results may differ from a plain program's by a relative error of at most 0.0003.
Values sent between devices are 32-bit elements; how exact they have to be, the bound alone decides.
No kernel may reach another device: no remote copies, remote signals or barrier semaphores. Data moves between devices by JAX's collectives and lax.ppermute only.
A program may use at most 64 MiB of HBM per device.

v0:
```python
import jax
import jax.numpy as jnp
from jax import lax
from jax.sharding import PartitionSpec as P

forch_coeff = 0.55
time_step = 500.0


def padded_2(block, sides, width):
    for axis, dim in sides:
        count = lax.axis_size(axis)
        forward = [(i, i + 1) for i in range(count - 1)]
        backward = [(target, source) for source, target in forward]
        low = lax.ppermute(
            lax.slice_in_dim(block, block.shape[dim] - width, None, axis=dim), axis, forward
        )
        high = lax.ppermute(lax.slice_in_dim(block, 0, width, axis=dim), axis, backward)
        block = jnp.concatenate([low, block, high], axis=dim)
    return block


def harmonic(first, second):
    return 2.0 * first * second / (first + second)


def mobility(permeability, speed):
    perm_cells = permeability.astype(jnp.float32)
    return perm_cells / (1.0 + forch_coeff * jnp.sqrt(perm_cells) * speed.astype(jnp.float32))


def segment_reduce(lower, main, upper, right_side):
    count = lower.shape[0]
    inner_low = lower[1 : count - 1].at[0].set(0.0)
    inner_up = upper[1 : count - 1].at[-1].set(0.0)
    inner_main = main[1 : count - 1]
    zeros_inner = jnp.zeros_like(inner_main)
    left_col = zeros_inner.at[0].set(-lower[1])
    right_col = zeros_inner.at[-1].set(-upper[count - 2])
    columns = jnp.stack([right_side[1 : count - 1], left_col, right_col], 1)

    def forward(carry, row):
        ratio_prev, value_prev = carry
        low_row, main_row, up_row, rhs_row = row
        divisor = main_row - low_row * ratio_prev
        ratio = up_row / divisor
        value = (rhs_row - low_row[None] * value_prev) / divisor[None]
        return ((ratio, value), (ratio, value))

    start = (jnp.zeros_like(inner_main[0]), jnp.zeros_like(columns[0]))
    _, (ratios, values) = lax.scan(forward, start, (inner_low, inner_main, inner_up, columns))

    def backward(after, row):
        ratio, value = row
        result = value - ratio[None] * after
        return (result, result)

    _, solved = lax.scan(backward, jnp.zeros_like(columns[0]), (ratios, values), reverse=True)
    base = solved[:, 0]
    from_first = solved[:, 1]
    from_last = solved[:, 2]
    diag_first = main[0] + upper[0] * from_first[0]
    diag_last = main[-1] + lower[-1] * from_last[-1]
    alphas = jnp.stack([lower[0] / diag_first, lower[-1] * from_first[-1] / diag_last])
    gammas = jnp.stack([upper[0] * from_last[0] / diag_first, upper[-1] / diag_last])
    deltas = jnp.stack(
        [
            (right_side[0] - upper[0] * base[0]) / diag_first,
            (right_side[-1] - lower[-1] * base[-1]) / diag_last,
        ]
    )
    return (jnp.stack([alphas, gammas, deltas]), (base, from_first, from_last))


def reduce_update(own, below, above):
    divisor = 1.0 - own[0] * below[1] - own[1] * above[0]
    new_alpha = -own[0] * below[0] / divisor
    new_gamma = -own[1] * above[1] / divisor
    new_delta = (own[2] - own[0] * below[2] - own[1] * above[2]) / divisor
    return jnp.stack([new_alpha, new_gamma, new_delta])


def reduce_local(reduced):
    rows = reduced.shape[1]
    for level in range(rows.bit_length() - 1):
        stride = 1 << level
        blank = jnp.zeros_like(reduced[:, :stride])
        below = jnp.concatenate([blank, reduced[:, :-stride]], 1)
        above = jnp.concatenate([reduced[:, stride:], blank], 1)
        reduced = reduce_update(reduced, below, above)
    return reduced[2]


def interface_x(reduced):
    whole = lax.all_gather(reduced, "gx", axis=1, tiled=True)
    solved = reduce_local(whole)
    return lax.dynamic_slice_in_dim(solved, 2 * lax.axis_index("gx"), 2, 0)


def interface_y(reduced):
    whole = lax.all_gather(reduced, "gy", axis=1, tiled=True)
    solved = reduce_local(whole)
    return lax.dynamic_slice_in_dim(solved, 2 * lax.axis_index("gy"), 2, 0)


def partitioned(lower, main, upper, right_side, interface):
    reduced, pieces = segment_reduce(lower, main, upper, right_side)
    ends = interface(reduced)
    first_row = ends[0]
    last_row = ends[1]
    inner = pieces[0] + pieces[1] * first_row[None] + pieces[2] * last_row[None]
    return jnp.concatenate([first_row[None], inner, last_row[None]], 0)


def local(pressure, source, porosity, permeability, speed):
    cells_x, cells_y, cells_z = pressure.shape
    mobility_field = mobility(permeability, speed)
    stacked = jnp.stack([mobility_field, pressure])
    padded = padded_2(stacked, (("gy", 2), ("gx", 1)), 1)
    padded_mob = jnp.pad(padded[0], ((0, 0), (0, 0), (1, 1)))
    padded_p = jnp.pad(padded[1], ((0, 0), (0, 0), (1, 1)))
    face_xp = harmonic(mobility_field, padded_mob[2:, 1:-1, 1:-1])
    face_xm = harmonic(mobility_field, padded_mob[:-2, 1:-1, 1:-1])
    face_yp = harmonic(mobility_field, padded_mob[1:-1, 2:, 1:-1])
    face_ym = harmonic(mobility_field, padded_mob[1:-1, :-2, 1:-1])
    face_zp = harmonic(mobility_field, padded_mob[1:-1, 1:-1, 2:])
    face_zm = harmonic(mobility_field, padded_mob[1:-1, 1:-1, :-2])
    laplacian = face_xp * (padded_p[2:, 1:-1, 1:-1] - pressure) + face_xm * (
        padded_p[:-2, 1:-1, 1:-1] - pressure
    )
    laplacian = (
        laplacian
        + face_yp * (padded_p[1:-1, 2:, 1:-1] - pressure)
        + face_ym * (padded_p[1:-1, :-2, 1:-1] - pressure)
    )
    laplacian = (
        laplacian
        + face_zp * (padded_p[1:-1, 1:-1, 2:] - pressure)
        + face_zm * (padded_p[1:-1, 1:-1, :-2] - pressure)
    )
    residual_field = laplacian - source
    ratio_field = porosity.astype(jnp.float32) / time_step

    def flat_x(values):
        return values.reshape(cells_x, cells_y * cells_z)

    def flat_y(values):
        return jnp.transpose(values, (1, 0, 2)).reshape(cells_y, cells_x * cells_z)

    along_x = partitioned(
        flat_x(-face_xm),
        flat_x(ratio_field + face_xm + face_xp),
        flat_x(-face_xp),
        flat_x(residual_field),
        interface_x,
    )
    along_x = along_x.reshape(cells_x, cells_y, cells_z)
    correction = partitioned(
        flat_y(-face_ym),
        flat_y(ratio_field + face_ym + face_yp),
        flat_y(-face_yp),
        flat_y(ratio_field * along_x),
        interface_y,
    )
    correction = jnp.transpose(correction.reshape(cells_y, cells_x, cells_z), (1, 0, 2))
    return pressure + correction


def solution(mesh):
    in_specs = (
        P("gx", "gy", None),
        P("gx", "gy", None),
        P("gx", "gy", None),
        P("gx", "gy", None),
        P("gx", "gy", None),
    )
    out_specs = P("gx", "gy", None)
    return jax.shard_map(local, mesh=mesh, in_specs=in_specs, out_specs=out_specs, check_vma=False)
```

profile of v0, /device:TPU:1, one launch (start us, length us, event | category | flops | bytes accessed | tf_op | source)
XLA Modules:
  0.0 180.4 jit_solution(4275080858047885994)
XLA Ops:
  6.5 1.0 fusion.185
  7.5 0.9 pad_maximum_fusion.17
  8.4 4.6 %collective-permute-start = (f32[2,16,1,128]{3,2,1,0:T(1,128)S(1)}, f32[2,16,1,128]{3,2,1,0:T(1,128)S(1)}, u32[]{:S(2)}, u32[]{:S(2)}) collective-permute-start(f32[2,16,1,128]{3,2,1,0:T(1,128)S(1)} %get-tuple-element.677), channel_id=1, source_target_pairs={{0,32},{32,64},{64,96},{96,128},{128,160},{160,192},{192,224},{224... | collective-permute-start | bytes 49160 | tf_op jit(solution)/shard_map/ppermute | solution.py:15
  13.0 5.5 %collective-permute-start.1 = (f32[2,16,1,128]{3,2,1,0:T(1,128)S(1)}, f32[2,16,1,128]{3,2,1,0:T(1,128)S(1)}, u32[]{:S(2)}, u32[]{:S(2)}) collective-permute-start(f32[2,16,1,128]{3,2,1,0:T(1,128)S(1)} %get-tuple-element.678), channel_id=1, source_target_pairs={{32,0},{64,32},{96,64},{128,96},{160,128},{192,160},{224,192},{256... | collective-permute-start | bytes 49160 | tf_op jit(solution)/shard_map/ppermute | solution.py:18
  18.5 0.8 collective-permute-done.1
  19.3 0.7 pad_maximum_fusion.15
  20.1 1.9 %collective-permute-start.2 = (f32[2,1,18,128]{3,2,1,0:T(8,128)S(1)}, f32[2,1,18,128]{3,2,1,0:T(8,128)S(1)}, u32[]{:S(2)}, u32[]{:S(2)}) collective-permute-start(f32[2,1,18,128]{3,2,1,0:T(8,128)S(1)} %get-tuple-element.675), channel_id=1, source_target_pairs={{0,1},{1,2},{2,3},{3,4},{4,5},{5,6},{6,7},{7,8},{8,9},{9,10},{10,1... | collective-permute-start | bytes 55304 | tf_op jit(solution)/shard_map/ppermute | solution.py:15
  21.9 1.3 collective-permute-start.3
  23.3 3.6 %collective-permute-done.3 = f32[2,1,18,128]{3,2,1,0:T(8,128)S(1)} collective-permute-done((f32[2,1,18,128]{3,2,1,0:T(8,128)S(1)}, f32[2,1,18,128]{3,2,1,0:T(8,128)S(1)}, u32[]{:S(2)}, u32[]{:S(2)}) %collective-permute-start.3) | collective-permute-done | bytes 18464 | tf_op jit(solution)/shard_map/ppermute | solution.py:18
  26.8 1.0 pad_maximum_fusion.9
  27.9 0.2 add_add_fusion
  28.2 0.6 copy-done.1
  28.8 0.4 fusion.128
  30.1 4.8 %while.76 = (s32[]{:T(128)}, f32[2048]{0:T(1024)S(1)}, f32[3,2048]{1,0:T(4,128)S(1)}, f32[14,2048]{1,0:T(8,128)S(1)}, f32[14,3,2048]{2,1,0:T(4,128)S(1)}, /*inde...) while((s32[]{:T(128)}, f32[2048]{0:T(1024)S(1)}, ...), condition=%wide.region_1.2_spmd.clone, body=%wide.region_0.1_spmd.clone.sunk | while | flops 32771 | bytes 262280 | solution.py:51
  30.6 0.2 dynamic_update_slice.49
  31.3 0.2 dynamic_update_slice.49
  32.0 0.2 dynamic_update_slice.49
  32.7 0.2 dynamic_update_slice.49
  33.4 0.2 dynamic_update_slice.49
  35.0 1.1 while.77
  36.4 0.7 pad_maximum_fusion.10
  37.9 0.4 scatter.29
  38.5 85.9 %all-gather.2.cloned.1.call-done = f32[3,64,2048]{2,0,1:T(4,128)} async-done(((f32[3,2,2048]{2,0,1:T(4,128)}), f32[3,64,2048]{2,0,1:T(4,128)}) %all-gather.2.cloned.1.call-update) | async-done | bytes 1572880 | tf_op jit(solution)/shard_map/all_gather | solution.py:95
  124.4 3.0 %fusion.196 = (f32[3,63,2048]{2,0,1:T(4,128)S(1)}, f32[3,63,2048]{2,0,1:T(4,128)S(1)}) fusion(f32[3,64,2048]{2,0,1:T(4,128)} %all-gather.2.cloned.1.call-done), kind=kLoop, calls=%fused_computation.379 | loop fusion | bytes 6193152 | tf_op jit(solution)/shard_map/slice | solution.py:89
  127.4 0.9 copy.125
  128.3 0.9 copy.127
  129.2 0.7 copy-done
  129.9 1.1 fusion.195
  131.0 1.0 fusion.16
  132.1 0.3 fusion.201
  132.4 0.6 fusion.29
  133.1 0.3 fusion.200
  133.4 0.6 fusion.38
  134.1 0.3 fusion.199
  134.6 0.3 fusion.46
  135.1 0.3 fusion.198
  135.5 0.5 fusion.63
  137.1 4.8 %while.78 = (s32[]{:T(128)}, f32[2048]{0:T(1024)S(1)}, f32[3,2048]{1,0:T(4,128)S(1)}, f32[14,2048]{1,0:T(8,128)S(1)}, f32[14,3,2048]{2,1,0:T(4,128)S(1)}, /*inde...) while((s32[]{:T(128)}, f32[2048]{0:T(1024)S(1)}, ...), condition=%wide.region_5.6_spmd.clone, body=%wide.region_4.5_spmd.clone.sunk | while | flops 32771 | bytes 262280 | solution.py:51
  142.0 1.1 while.79
  143.4 24.7 %all_gather.7 = f32[3,32,2048]{2,0,1:T(4,128)S(1)} all-gather(f32[3,2,2048]{2,0,1:T(4,128)S(1)} %pad_maximum_fusion.11), channel_id=1, replica_groups=mesh['gy'=16,'gx'=32] {'gy'}, dimensions={1}, use_global_device_ids=true | all-gather | bytes 835584 | tf_op jit(solution)/shard_map/all_gather | solution.py:101
  168.1 0.7 fusion.203
  168.8 0.6 fusion.202
  169.7 0.4 copy.130
  170.1 0.4 copy.132
  170.6 0.5 fusion.77
  171.3 0.2 fusion.90
  171.8 0.2 fusion.103
  172.8 0.7 copy.120
  (306 shorter events, 14.3 us)
Async XLA Ops:
  6.5 21.3 %copy-start.3 = (bf16[16,16,128]{2,1,0:T(8,128)(2,1)S(1)}, bf16[16,16,128]{2,1,0:T(8,128)(2,1)}, u32[]{:S(2)}) copy-start(bf16[16,16,128]{2,1,0:T(8,128)(2,1)} %param.32) | copy-start | bytes 196612
  6.5 21.3 %copy-start.2 = (bf16[16,16,128]{2,1,0:T(8,128)(2,1)S(1)}, bf16[16,16,128]{2,1,0:T(8,128)(2,1)}, u32[]{:S(2)}) copy-start(bf16[16,16,128]{2,1,0:T(8,128)(2,1)} %param.33) | copy-start | bytes 196612
  6.5 21.4 %copy-start.4 = (bf16[16,16,128]{2,1,0:T(8,128)(2,1)S(1)}, bf16[16,16,128]{2,1,0:T(8,128)(2,1)}, u32[]{:S(2)}) copy-start(bf16[16,16,128]{2,1,0:T(8,128)(2,1)} %param.31) | copy-start | bytes 196612
  6.5 117.9 %all-gather.2.cloned.1.call-start = ((), (), s32[]{:S(2)}) async-start(), calls=%async_computation | async-start | bytes 2162688 | tf_op jit(solution)/shard_map/all_gather | solution.py:95
  8.4 10.1 %collective-permute-start = (f32[2,16,1,128]{3,2,1,0:T(1,128)S(1)}, f32[2,16,1,128]{3,2,1,0:T(1,128)S(1)}, u32[]{:S(2)}, u32[]{:S(2)}) collective-permute-start(f32[2,16,1,128]{3,2,1,0:T(1,128)S(1)} %get-tuple-element.677), channel_id=1, source_target_pairs={{0,32},{32,64},{64,96},{96,128},{128,160},{160,192},{192,224},{224... | collective-permute-start | bytes 49160 | tf_op jit(solution)/shard_map/ppermute | solution.py:15
  13.0 6.3 %collective-permute-start.1 = (f32[2,16,1,128]{3,2,1,0:T(1,128)S(1)}, f32[2,16,1,128]{3,2,1,0:T(1,128)S(1)}, u32[]{:S(2)}, u32[]{:S(2)}) collective-permute-start(f32[2,16,1,128]{3,2,1,0:T(1,128)S(1)} %get-tuple-element.678), channel_id=1, source_target_pairs={{32,0},{64,32},{96,64},{128,96},{160,128},{192,160},{224,192},{256... | collective-permute-start | bytes 49160 | tf_op jit(solution)/shard_map/ppermute | solution.py:18
  20.1 3.2 %collective-permute-start.2 = (f32[2,1,18,128]{3,2,1,0:T(8,128)S(1)}, f32[2,1,18,128]{3,2,1,0:T(8,128)S(1)}, u32[]{:S(2)}, u32[]{:S(2)}) collective-permute-start(f32[2,1,18,128]{3,2,1,0:T(8,128)S(1)} %get-tuple-element.675), channel_id=1, source_target_pairs={{0,1},{1,2},{2,3},{3,4},{4,5},{5,6},{6,7},{7,8},{8,9},{9,10},{10,1... | collective-permute-start | bytes 55304 | tf_op jit(solution)/shard_map/ppermute | solution.py:15
  21.9 4.9 %collective-permute-start.3 = (f32[2,1,18,128]{3,2,1,0:T(8,128)S(1)}, f32[2,1,18,128]{3,2,1,0:T(8,128)S(1)}, u32[]{:S(2)}, u32[]{:S(2)}) collective-permute-start(f32[2,1,18,128]{3,2,1,0:T(8,128)S(1)} %get-tuple-element.676), channel_id=1, source_target_pairs={{1,0},{2,1},{3,2},{4,3},{5,4},{6,5},{7,6},{8,7},{9,8},{10,9},{11,1... | collective-permute-start | bytes 55304 | tf_op jit(solution)/shard_map/ppermute | solution.py:18
  27.8 0.9 copy-start.1
  27.8 1.0 copy-start.5
  128.3 1.6 copy-start
Sparse Core Ops, SparseCore 0:
  37.2 87.1 all-gather.1
where the time goes:
time: 181 us; the launch traced here: 180 us
  waiting for transfers between devices  90.3 us (50%)
  blocking collectives  24.7 us (14%)
  local copies, waits for them, and re-layouts  21.9 us (12%)
  between operations  14.4 us (8%)
  other arithmetic  13.7 us (8%)
  starting transfers between devices  13.2 us (7%)
  loops' own time  2.15 us (1%)
    all_gather x1, waiting for transfers between devices, interface_x(): whole = lax.all_gather(reduced, 'gx', axis=1, tiled=True)  85.9 us
    all_gather x1, blocking collectives, interface_y(): whole = lax.all_gather(reduced, 'gy', axis=1, tiled=True)  24.7 us
    ppermute x2, starting transfers between devices, padded_2(): lax.ppermute(lax.slice_in_dim(block, 0, width, axis=dim), axis, backward)  6.77 us
    ppermute x2, starting transfers between devices, padded_2(): lax.ppermute(lax.slice_in_dim(block, block.shape[dim] - width, None, axis...  6.46 us
    dynamic_update_slice x28, local copies, waits for them, and re-layouts, segment_reduce(): lax.scan(forward, start, (inner_low, inner_main, inner_up, columns))  5.72 us
    slice x8, local copies, waits for them, and re-layouts, reduce_local(): above = jnp.concatenate([reduced[:, stride:], blank], 1)  4.96 us
    unnamed x30, local copies, waits for them, and re-layouts  4.39 us
    ppermute x2, waiting for transfers between devices, padded_2(): lax.ppermute(lax.slice_in_dim(block, 0, width, axis=dim), axis, backward)  4.37 us
  transfers between devices with their start and end apart: 5, of which 3 were waited for; matrix products, arithmetic and copies ran while one was open for 1% of the time, Pallas kernels for 0%

commit v1 on v0

v1 whole, which is shorter than its diff:
```python
import jax
import jax.numpy as jnp
from jax import lax
from jax.experimental import pallas as pl
from jax.experimental.pallas import tpu as pltpu
from jax.sharding import PartitionSpec as P

FORCH = 0.55
STEP = 500.0
NEAR_X = 4
NEAR_Y = 2
F32 = jnp.float32


def join(left, right):
    la, lb, lc, lg, lh = left
    ra, rb, rc, rg, rh = right
    inv = 1.0 / (lc + ra)
    left_share = lb * inv
    right_share = rb * inv
    gap = lh - rg
    merged = (
        la - lb * left_share,
        lb * right_share,
        rc - rb * right_share,
        lg - left_share * gap,
        rh + right_share * gap,
    )
    return merged, (inv * gap, left_share, right_share)


def join_all(pieces):
    if len(pieces) == 1:
        return pieces[0], None
    half = len(pieces) // 2
    left, left_tree = join_all(pieces[:half])
    right, right_tree = join_all(pieces[half:])
    merged, face = join(left, right)
    return merged, (face, left_tree, right_tree)


def face_fluxes(tree, low, high):
    if tree is None:
        return [low, high]
    face, left_tree, right_tree = tree
    flux = face[0]
    if low is not None:
        flux = flux + face[1] * low
    if high is not None:
        flux = flux + face[2] * high
    return face_fluxes(left_tree, low, flux) + face_fluxes(right_tree, flux, high)[1:]


def tree_shape(count):
    if count == 1:
        return None
    return (count, tree_shape(count // 2), tree_shape(count // 2))


def tree_values(tree):
    if tree is None:
        return []
    return list(tree[0]) + tree_values(tree[1]) + tree_values(tree[2])


def tree_of(shape, values):
    if shape is None:
        return None
    face = tuple(values.pop(0) for _ in range(3))
    left = tree_of(shape[1], values)
    return (face, left, tree_of(shape[2], values))


def plane(ref, i, rows):
    return ref[i * rows : (i + 1) * rows, :]


def eliminate(ratio, half, count):
    gaps = [half[i] + half[i + 1] for i in range(count - 1)]
    up = []
    total = ratio[0]
    for i in range(count - 1):
        carry = 1.0 / (1.0 + total * gaps[i])
        up.append(carry)
        total = ratio[i + 1] + total * carry
    last_inv = 1.0 / total
    down = [None] * (count - 1)
    total = ratio[count - 1]
    for i in range(count - 2, -1, -1):
        carry = 1.0 / (1.0 + total * gaps[i])
        down[i] = carry
        total = ratio[i] + total * carry
    first_inv = 1.0 / total
    across = last_inv
    for i in range(count - 2, -1, -1):
        across = across * up[i]
    ends = [first_inv + half[0], across, last_inv + half[count - 1], first_inv, last_inv]
    return gaps, up, down, ends


def offsets(right, up, down, first_inv, last_inv, count):
    rising = right[0]
    for i in range(count - 1):
        rising = right[i + 1] + up[i] * rising
    falling = right[count - 1]
    for i in range(count - 2, -1, -1):
        falling = right[i] + down[i] * falling
    return falling * first_inv, rising * last_inv


def substitute(right, gaps, up, last_inv, low, high, count):
    sums = [right[0] + low]
    for i in range(count - 1):
        sums.append(right[i + 1] + up[i] * sums[i])
    values = [None] * count
    values[count - 1] = (sums[count - 1] - high) * last_inv
    for i in range(count - 2, -1, -1):
        values[i] = up[i] * (values[i + 1] + gaps[i] * sums[i])
    return values


def local_step(sizes, sizes_mesh, pressure, source, porosity, permeability, speed):
    nx, ny, nz = sizes
    count_gx, count_gy = sizes_mesh
    far_x = count_gx // NEAR_X
    far_y = count_gy // NEAR_Y
    near_x_groups = [[z * NEAR_X + x for x in range(NEAR_X)] for z in range(far_x)]
    far_x_groups = [[z * NEAR_X + x for z in range(far_x)] for x in range(NEAR_X)]
    far_y_groups = [[y * NEAR_Y + c for y in range(far_y)] for c in range(NEAR_Y)]
    cells = nx * ny
    pressure = pressure.reshape(cells, nz)
    source = source.reshape(cells, nz)
    porosity = porosity.reshape(cells, nz)
    permeability = permeability.reshape(cells, nz)
    speed = speed.reshape(cells, nz)

    def call(body, shapes, scratch, *args, name):
        return pl.pallas_call(
            body,
            out_shape=[jax.ShapeDtypeStruct(s, F32) for s in shapes],
            in_specs=[pl.BlockSpec(memory_space=pltpu.VMEM)] * len(args),
            out_specs=[pl.BlockSpec(memory_space=pltpu.VMEM)] * len(shapes),
            scratch_shapes=[pltpu.VMEM(s, F32) for s in scratch],
            compiler_params=pltpu.CompilerParams(vmem_limit_bytes=32 * 1024 * 1024),
            name=name,
        )(*args)

    def rows_y(ref, j):
        return ref[pl.ds(j, nx, stride=ny), :]

    def halves_body(perm_ref, speed_ref, p_ref, half_ref, near_ref, far_ref):
        for i in range(nx):
            root = lax.rsqrt(plane(perm_ref, i, ny).astype(F32))
            half_ref[i * ny : (i + 1) * ny, :] = (0.5 * root) * (
                root + FORCH * plane(speed_ref, i, ny).astype(F32)
            )
        even = lax.rem(lax.axis_index("gy"), 2) == 0
        for k, ref in enumerate((half_ref, p_ref)):
            low = rows_y(ref, 0)
            high = rows_y(ref, ny - 1)
            near_ref[k] = jnp.where(even, high, low)
            far_ref[k] = jnp.where(even, low, high)

    half, near_send, far_send = call(
        halves_body, [(cells, nz), (2, nx, nz), (2, nx, nz)], [], permeability, speed, pressure,
        name="halves",
    )
    far_pairs = []
    for i in range(1, count_gy - 1, 2):
        far_pairs += [(i, i + 1), (i + 1, i)]
    far_got = lax.ppermute(far_send, "gy", far_pairs)
    near_got = lax.ppermute(near_send, "gy", [(i, i ^ 1) for i in range(count_gy)])

    def inner_body(
        p_ref, source_ref, por_ref, half_ref,
        right_ref, ratio_ref, xup_ref, xdown_ref, xends_ref, yup_ref, ydown_ref, yends_ref,
    ):
        lane = lax.broadcasted_iota(jnp.int32, (ny, nz), 1)
        row = lax.broadcasted_iota(jnp.int32, (ny, nz), 0)
        for i in range(nx):
            p = plane(p_ref, i, ny)
            h = plane(half_ref, i, ny)
            ratio = plane(por_ref, i, ny).astype(F32) * (1.0 / STEP)
            ratio_ref[i * ny : (i + 1) * ny, :] = ratio
            flux_z = (pltpu.roll(p, nz - 1, 1) - p) / (pltpu.roll(h, nz - 1, 1) + h)
            flux_z = jnp.where(lane == nz - 1, 0.0, flux_z)
            flux_y = (pltpu.roll(p, ny - 1, 0) - p) / (pltpu.roll(h, ny - 1, 0) + h)
            flux_y = jnp.where(row == ny - 1, 0.0, flux_y)
            lap = (flux_z - pltpu.roll(flux_z, 1, 1)) + (flux_y - pltpu.roll(flux_y, 1, 0))
            right_ref[i * ny : (i + 1) * ny, :] = (lap - plane(source_ref, i, ny)) + ratio * p
        ratios = [plane(ratio_ref, i, ny) for i in range(nx)]
        halves = [plane(half_ref, i, ny) for i in range(nx)]
        _, up, down, ends = eliminate(ratios, halves, nx)
        for i in range(nx - 1):
            xup_ref[i] = up[i]
            xdown_ref[i] = down[i]
        for k in range(5):
            xends_ref[k] = ends[k]
        ratios = [rows_y(ratio_ref, j) for j in range(ny)]
        halves = [rows_y(half_ref, j) for j in range(ny)]
        _, up, down, ends = eliminate(ratios, halves, ny)
        for j in range(ny - 1):
            yup_ref[j] = up[j]
            ydown_ref[j] = down[j]
        for k in range(5):
            yends_ref[k] = ends[k]

    right0, ratio, xup, xdown, xends, yup, ydown, yends = call(
        inner_body,
        [
            (cells, nz), (cells, nz), (nx - 1, ny, nz), (nx - 1, ny, nz), (5, ny, nz),
            (ny - 1, nx, nz), (ny - 1, nx, nz), (5, nx, nz),
        ],
        [], pressure, source, porosity, half, name="inner",
    )

    def edges_body(
        right0_ref, p_ref, half_ref, near_ref, far_ref, xup_ref, xdown_ref, xends_ref, right_ref, send_ref
    ):
        place = lax.axis_index("gy")
        even = lax.rem(place, 2) == 0
        right_ref[...] = right0_ref[...]
        for j, is_end, low in ((0, place == 0, True), (ny - 1, place == count_gy - 1, False)):
            first, second = (far_ref, near_ref) if low else (near_ref, far_ref)
            other_h = jnp.where(even, first[0], second[0])
            other_p = jnp.where(even, first[1], second[1])
            flux = (other_p - rows_y(p_ref, j)) / (other_h + rows_y(half_ref, j))
            flux = jnp.where(is_end, 0.0, flux)
            right_ref[pl.ds(j, nx, stride=ny), :] = rows_y(right_ref, j) + flux
        right = [plane(right_ref, i, ny) for i in range(nx)]
        up = [xup_ref[i] for i in range(nx - 1)]
        down = [xdown_ref[i] for i in range(nx - 1)]
        first, last = offsets(right, up, down, xends_ref[3], xends_ref[4], nx)
        for k, value in enumerate((xends_ref[0], xends_ref[1], xends_ref[2], first, last)):
            for target in range(NEAR_X):
                send_ref[target, k] = value

    right, near_x = call(
        edges_body, [(cells, nz), (NEAR_X, 5, ny, nz)], [],
        right0, pressure, half, near_got, far_got, xup, xdown, xends, name="edges",
    )
    near_x = lax.all_to_all(near_x, "gx", 0, 0, axis_index_groups=near_x_groups)

    def ring_body(got_ref, send_ref, tree_ref):
        pieces = [tuple(got_ref[n, k] for k in range(5)) for n in range(NEAR_X)]
        merged, tree = join_all(pieces)
        for k in range(5):
            for target in range(far_x):
                send_ref[target, k] = merged[k]
        for k, value in enumerate(tree_values(tree)):
            tree_ref[k] = value

    far_x_send, x_tree = call(
        ring_body, [(far_x, 5, ny, nz), (3 * (NEAR_X - 1), ny, nz)], [], near_x, name="x_ring"
    )
    far_x_got = lax.all_to_all(far_x_send, "gx", 0, 0, axis_index_groups=far_x_groups)

    def along_x_body(
        got_ref, tree_ref, right_ref, half_ref, ratio_ref, p_ref, xup_ref, xends_ref,
        yup_ref, ydown_ref, yends_ref,
        send_ref, yright_ref, far_faces, near_faces, solved_ref,
    ):
        place = lax.axis_index("gx")
        far = place // NEAR_X
        near = lax.rem(place, NEAR_X)
        pieces = [tuple(got_ref[n, k] for k in range(5)) for n in range(far_x)]
        _, tree = join_all(pieces)
        fluxes = face_fluxes(tree, None, None)
        zero = jnp.zeros((ny, nz), F32)
        for k, value in enumerate(fluxes):
            far_faces[k] = zero if value is None else value
        low = far_faces[far]
        high = far_faces[far + 1]
        tree = tree_of(tree_shape(NEAR_X), [tree_ref[k] for k in range(3 * (NEAR_X - 1))])
        for k, value in enumerate(face_fluxes(tree, low, high)):
            near_faces[k] = value
        low = near_faces[near]
        high = near_faces[near + 1]
        gaps = [plane(half_ref, i, ny) + plane(half_ref, i + 1, ny) for i in range(nx - 1)]
        up = [xup_ref[i] for i in range(nx - 1)]
        right = [plane(right_ref, i, ny) for i in range(nx)]
        values = substitute(right, gaps, up, xends_ref[4], low, high, nx)
        for i in range(nx):
            solved_ref[i * ny : (i + 1) * ny, :] = plane(ratio_ref, i, ny) * (values[i] - plane(p_ref, i, ny))
        yright = [rows_y(solved_ref, j) for j in range(ny)]
        for j in range(ny):
            yright_ref[j] = yright[j]
        up = [yup_ref[j] for j in range(ny - 1)]
        down = [ydown_ref[j] for j in range(ny - 1)]
        first, last = offsets(yright, up, down, yends_ref[3], yends_ref[4], ny)
        for k, value in enumerate((yends_ref[0], yends_ref[1], yends_ref[2], first, last)):
            send_ref[k] = value

    pair_send, yright = call(
        along_x_body,
        [(5, nx, nz), (ny, nx, nz)],
        [(far_x + 1, ny, nz), (NEAR_X + 1, ny, nz), (cells, nz)],
        far_x_got, x_tree, right, half, ratio, pressure, xup, xends, yup, ydown, yends,
        name="along_x",
    )
    pair_got = lax.ppermute(pair_send, "gy", [(i, i ^ 1) for i in range(count_gy)])

    def pair_body(own_ref, got_ref, send_ref, tree_ref):
        even = lax.rem(lax.axis_index("gy"), 2) == 0
        left = tuple(jnp.where(even, own_ref[k], got_ref[k]) for k in range(5))
        right = tuple(jnp.where(even, got_ref[k], own_ref[k]) for k in range(5))
        merged, face = join(left, right)
        for k in range(5):
            for target in range(far_y):
                send_ref[target, k] = merged[k]
        for k in range(3):
            tree_ref[k] = face[k]

    far_y_send, y_tree = call(
        pair_body, [(far_y, 5, nx, nz), (3, nx, nz)], [], pair_send, pair_got, name="y_pair"
    )
    far_y_got = lax.all_to_all(far_y_send, "gy", 0, 0, axis_index_groups=far_y_groups)

    def updated_body(
        got_ref, tree_ref, yright_ref, half_ref, p_ref, yup_ref, yends_ref, out_ref, far_faces, near_faces
    ):
        place = lax.axis_index("gy")
        far = place // NEAR_Y
        near = lax.rem(place, NEAR_Y)
        pieces = [tuple(got_ref[n, k] for k in range(5)) for n in range(far_y)]
        _, tree = join_all(pieces)
        zero = jnp.zeros((nx, nz), F32)
        for k, value in enumerate(face_fluxes(tree, None, None)):
            far_faces[k] = zero if value is None else value
        low = far_faces[far]
        high = far_faces[far + 1]
        tree = tree_of(tree_shape(NEAR_Y), [tree_ref[k] for k in range(3)])
        for k, value in enumerate(face_fluxes(tree, low, high)):
            near_faces[k] = value
        low = near_faces[near]
        high = near_faces[near + 1]
        halves = [rows_y(half_ref, j) for j in range(ny)]
        gaps = [halves[j] + halves[j + 1] for j in range(ny - 1)]
        up = [yup_ref[j] for j in range(ny - 1)]
        right = [yright_ref[j] for j in range(ny)]
        values = substitute(right, gaps, up, yends_ref[4], low, high, ny)
        for j in range(ny):
            out_ref[pl.ds(j, nx, stride=ny), :] = rows_y(p_ref, j) + values[j]

    (updated,) = call(
        updated_body,
        [(cells, nz)],
        [(far_y + 1, nx, nz), (NEAR_Y + 1, nx, nz)],
        far_y_got, y_tree, yright, half, pressure, yup, yends,
        name="updated",
    )
    return updated.reshape(nx, ny, nz)


def solution(mesh):
    spec = P("gx", "gy", None)
    sizes_mesh = (mesh.shape["gx"], mesh.shape["gy"])

    def local(pressure, source, porosity, permeability, speed):
        return local_step(
            pressure.shape, sizes_mesh, pressure, source, porosity, permeability, speed
        )

    return jax.shard_map(
        local, mesh=mesh, in_specs=(spec,) * 5, out_specs=spec, check_vma=False
    )
```

time: 181 us -> 68.2 us (0.38)
  waiting for transfers between devices: 90.3 us -> 3.07 us
  blocking collectives: 24.7 us -> 46.9 us
  local copies, waits for them, and re-layouts: 21.9 us -> 3.42 us
  between operations: 14.4 us -> 0.09 us
  other arithmetic: 13.7 us -> 0 us
  loops' own time: 2.15 us -> 0 us
    all_gather x1 -> x0, waiting for transfers between devices: 85.9 us -> none  [interface_x(): whole = lax.all_gather(reduced, 'gx', axis=1, tiled=True)]
    all_to_all x0 -> x3, blocking collectives: none -> 46.9 us  [the longest x1 21 us: local_step(): lax.all_to_all(far_y_send, 'gy', 0, 0, axis_index_groups=far_y_groups)]
    all_gather x1 -> x0, blocking collectives: 24.7 us -> none  [interface_y(): whole = lax.all_gather(reduced, 'gy', axis=1, tiled=True)]
    slice x31 -> x0, local copies, waits for them, and re-layouts: 7.57 us -> none  [the longest x8 4.96 us: reduce_local(): above = jnp.concatenate([reduced[:, stride:], blank], 1)]
    dynamic_update_slice x28 -> x0, local copies, waits for them, and re-layouts: 5.72 us -> none  [segment_reduce(): lax.scan(forward, start, (inner_low, inner_main, inner_up, columns))]
    div x41 -> x0, other arithmetic: 4.23 us -> none  [the longest x5 2.49 us: reduce_update(): new_gamma = -own[1] * above[1] / divisor]
    another operation x20 -> x0, other arithmetic: 2.84 us -> none  [the longest x1 0.98 us: local(): stacked = jnp.stack([mobility_field, pressure])]
    dynamic_update_slice x56 -> x0, other arithmetic: 2.34 us -> none  [segment_reduce(): lax.scan(forward, start, (inner_low, inner_main, inner_up, columns))]
  transfers between devices with their start and end apart: 5 -> 3, of which waited for: 3 -> 2; matrix products, arithmetic and copies ran while one was open for 1% -> 0% of each run, Pallas kernels for 0% -> 1%
where the time goes in v1:
time: 68.2 us; the launch traced here: 67.8 us
  blocking collectives  46.9 us (69%)
  starting transfers between devices  12.8 us (19%)
  local copies, waits for them, and re-layouts  3.42 us (5%)
  waiting for transfers between devices  3.07 us (5%)
  Pallas kernels  1.58 us (2%)
    all_to_all x1, blocking collectives, local_step(): lax.all_to_all(far_y_send, 'gy', 0, 0, axis_index_groups=far_y_groups)  21 us
    all_to_all x1, blocking collectives, local_step(): lax.all_to_all(far_x_send, 'gx', 0, 0, axis_index_groups=far_x_groups)  18.5 us
    ppermute x1, starting transfers between devices, local_step(): lax.ppermute(near_send, 'gy', [(i, i ^ 1) for i in range(count_gy)])  8.92 us
    all_to_all x1, blocking collectives, local_step(): near_x = lax.all_to_all(near_x, 'gx', 0, 0, axis_index_groups=near_x_groups)  7.36 us
    unnamed x12, local copies, waits for them, and re-layouts  3.42 us
    ppermute x1, starting transfers between devices, local_step(): lax.ppermute(pair_send, 'gy', [(i, i ^ 1) for i in range(count_gy)])  1.92 us
    ppermute x1, starting transfers between devices, local_step(): far_got = lax.ppermute(far_send, 'gy', far_pairs)  1.92 us
    ppermute x1, waiting for transfers between devices, local_step(): far_got = lax.ppermute(far_send, 'gy', far_pairs)  1.88 us
  transfers between devices with their start and end apart: 3, of which 2 were waited for; matrix products, arithmetic and copies ran while one was open for 0% of the time, Pallas kernels for 1%

profile of v1, /device:TPU:1, one launch (start us, length us, event | category | flops | bytes accessed | tf_op | source)
XLA Modules:
  0.0 67.8 jit_solution(12735794499720882867)
XLA Ops:
  0.0 0.0 copy-start
  0.0 0.9 %copy-done = f32[16,16,128]{2,1,0:T(8,128)S(1)} copy-done((f32[16,16,128]{2,1,0:T(8,128)S(1)}, f32[16,16,128]{2,1,0:T(8,128)}, u32[]{:S(2)}) %copy-start) | copy-done | bytes 131096
  0.9 0.0 copy-start.4
  0.9 0.8 %copy-done.4 = bf16[16,16,128]{2,1,0:T(8,128)(2,1)S(1)} copy-done((bf16[16,16,128]{2,1,0:T(8,128)(2,1)S(1)}, bf16[16,16,128]{2,1,0:T(8,128)(2,1)}, u32[]{:S(2)}) %copy-start.4) | copy-done | bytes 65560
  1.7 0.0 copy-start.5
  1.7 0.8 %copy-done.5 = bf16[16,16,128]{2,1,0:T(8,128)(2,1)S(1)} copy-done((bf16[16,16,128]{2,1,0:T(8,128)(2,1)S(1)}, bf16[16,16,128]{2,1,0:T(8,128)(2,1)}, u32[]{:S(2)}) %copy-start.5) | copy-done | bytes 65560
  2.6 0.0 copy-start.1
  2.6 0.0 copy-start.2
  2.6 8.9 %collective-permute-start = (f32[2,16,128]{2,1,0:T(8,128)S(1)}, f32[2,16,128]{2,1,0:T(8,128)S(1)}, u32[]{:S(2)}, u32[]{:S(2)}) collective-permute-start(f32[2,16,128]{2,1,0:T(8,128)S(1)} %get-tuple-element.26), channel_id=1, source_target_pairs={{0,32},{32,0},{64,96},{96,64},{128,160},{160,128},{192,224},{224,1... | collective-permute-start | bytes 49160 | tf_op jit(solution)/shard_map/ppermute | solution.py:172
  11.6 1.9 %collective-permute-start.1 = (f32[2,16,128]{2,1,0:T(8,128)S(1)}, f32[2,16,128]{2,1,0:T(8,128)S(1)}, u32[]{:S(2)}, u32[]{:S(2)}) collective-permute-start(f32[2,16,128]{2,1,0:T(8,128)S(1)} %get-tuple-element.27), channel_id=1, source_target_pairs={{32,64},{64,32},{96,128},{128,96},{160,192},{192,160},{224,256},{2... | collective-permute-start | bytes 49160 | tf_op jit(solution)/shard_map/ppermute | solution.py:171
  13.5 0.0 copy-done.1
  13.5 0.0 copy-done.2
  13.5 0.0 copy-start.3
  13.5 0.8 %copy-done.3 = bf16[16,16,128]{2,1,0:T(8,128)(2,1)S(1)} copy-done((bf16[16,16,128]{2,1,0:T(8,128)(2,1)S(1)}, bf16[16,16,128]{2,1,0:T(8,128)(2,1)}, u32[]{:S(2)}) %copy-start.3) | copy-done | bytes 65560
  14.4 0.4 inner.1
  14.7 0.0 collective-permute-done.near_ref
  14.7 1.9 %collective-permute-done.1.far_ref = f32[2,16,128]{2,1,0:T(8,128)S(1)} collective-permute-done((f32[2,16,128]{2,1,0:T(8,128)S(1)}, f32[2,16,128]{2,1,0:T(8,128)S(1)}, u32[]{:S(2)}, u32[]{:S(2)}) %collective-permute-start.1) | collective-permute-done | bytes 16416 | tf_op jit(solution)/shard_map/ppermute | solution.py:171
  16.6 0.1 edges.1
  16.7 7.4 %all_to_all.15.got_ref = f32[4,5,16,128]{3,2,1,0:T(8,128)S(1)} all-to-all(f32[4,5,16,128]{3,2,1,0:T(8,128)S(1)} %get-tuple-element.31), channel_id=1, replica_groups={{0,1,2,3},{4,5,6,7},{8,9,10,11},{12,13,14,15},{16,17,18,19},{20,21,22,2..., dimensions={0} | all-to-all | bytes 327680 | tf_op jit(solution)/shard_map/all_to_all | solution.py:242
  24.1 18.5 %all_to_all.16.got_ref = f32[8,5,16,128]{3,2,1,0:T(8,128)S(1)} all-to-all(f32[8,5,16,128]{3,2,1,0:T(8,128)S(1)} %get-tuple-element.32), channel_id=1, replica_groups={{0,4,8,12,16,20,24,28},{1,5,9,13,17,21,25,29},{2,6,10,14,18,22,26,30},{..., dimensions={0} | all-to-all | bytes 655360 | tf_op jit(solution)/shard_map/all_to_all | solution.py:256
  42.6 0.2 along_x.1
  42.8 1.9 %collective-permute-start.2 = (f32[5,16,128]{2,1,0:T(8,128)S(1)}, f32[5,16,128]{2,1,0:T(8,128)S(1)}, u32[]{:S(2)}, u32[]{:S(2)}) collective-permute-start(f32[5,16,128]{2,1,0:T(8,128)S(1)} %get-tuple-element.39.own_ref), channel_id=1, source_target_pairs={{0,32},{32,0},{64,96},{96,64},{128,160},{160,128},{192,224},{224,1... | collective-permute-start | bytes 122888 | tf_op jit(solution)/shard_map/ppermute | solution.py:301
  44.7 1.2 %collective-permute-done.2.got_ref = f32[5,16,128]{2,1,0:T(8,128)S(1)} collective-permute-done((f32[5,16,128]{2,1,0:T(8,128)S(1)}, f32[5,16,128]{2,1,0:T(8,128)S(1)}, u32[]{:S(2)}, u32[]{:S(2)}) %collective-permute-start.2) | collective-permute-done | bytes 40992 | tf_op jit(solution)/shard_map/ppermute | solution.py:301
  46.0 21.0 %all_to_all.17.got_ref = f32[8,5,16,128]{3,2,1,0:T(8,128)S(1)} all-to-all(f32[8,5,16,128]{3,2,1,0:T(8,128)S(1)} %get-tuple-element.40), channel_id=1, replica_groups={{0,64,128,192,256,320,384,448},{32,96,160,224,288,352,416,480},{1,65,12..., dimensions={0} | all-to-all | bytes 655360 | tf_op jit(solution)/shard_map/all_to_all | solution.py:317
  67.0 0.8 %updated.1 = f32[256,128]{1,0:T(8,128)} custom-call(f32[8,5,16,128]{3,2,1,0:T(8,128)S(1)} %all_to_all.17.got_ref, f32[3,16,128]{2,1,0:T(8,128)S(1)} %get-tuple-element.41.tree_ref, f32[16,16,128]{2,1,0:T(8,128)S(1)} %get-tuple-element.42.yright_ref, f32[256,128]{1,0:T(8,128)S(1)} %get-tuple-element.24.half_ref, f32[256,128]{1,0:T(8,128)S(1)} %bitcast.10, ...), custom_call_target="tpu_custom_call" | custom-call | tf_op jit(solution)/shard_map/updated/pallas_call | solution.py:138
  (3 shorter events, 0.1 us)
Async XLA Ops:
  0.0 0.9 %copy-start = (f32[16,16,128]{2,1,0:T(8,128)S(1)}, f32[16,16,128]{2,1,0:T(8,128)}, u32[]{:S(2)}) copy-start(f32[16,16,128]{2,1,0:T(8,128)} %param.5) | copy-start | bytes 393220
  0.9 0.8 %copy-start.4 = (bf16[16,16,128]{2,1,0:T(8,128)(2,1)S(1)}, bf16[16,16,128]{2,1,0:T(8,128)(2,1)}, u32[]{:S(2)}) copy-start(bf16[16,16,128]{2,1,0:T(8,128)(2,1)} %param.8) | copy-start | bytes 196612
  1.7 0.8 %copy-start.5 = (bf16[16,16,128]{2,1,0:T(8,128)(2,1)S(1)}, bf16[16,16,128]{2,1,0:T(8,128)(2,1)}, u32[]{:S(2)}) copy-start(bf16[16,16,128]{2,1,0:T(8,128)(2,1)} %param.9) | copy-start | bytes 196612
  2.6 10.9 %copy-start.1 = (f32[16,16,128]{2,1,0:T(8,128)S(1)}, f32[16,16,128]{2,1,0:T(8,128)}, u32[]{:S(2)}) copy-start(f32[16,16,128]{2,1,0:T(8,128)} %param.5) | copy-start | bytes 393220
  2.6 10.9 %copy-start.2 = (f32[16,16,128]{2,1,0:T(8,128)S(1)}, f32[16,16,128]{2,1,0:T(8,128)}, u32[]{:S(2)}) copy-start(f32[16,16,128]{2,1,0:T(8,128)} %param.6) | copy-start | bytes 393220
  2.6 12.1 %collective-permute-start = (f32[2,16,128]{2,1,0:T(8,128)S(1)}, f32[2,16,128]{2,1,0:T(8,128)S(1)}, u32[]{:S(2)}, u32[]{:S(2)}) collective-permute-start(f32[2,16,128]{2,1,0:T(8,128)S(1)} %get-tuple-element.26), channel_id=1, source_target_pairs={{0,32},{32,0},{64,96},{96,64},{128,160},{160,128},{192,224},{224,1... | collective-permute-start | bytes 49160 | tf_op jit(solution)/shard_map/ppermute | solution.py:172
  11.6 5.1 %collective-permute-start.1 = (f32[2,16,128]{2,1,0:T(8,128)S(1)}, f32[2,16,128]{2,1,0:T(8,128)S(1)}, u32[]{:S(2)}, u32[]{:S(2)}) collective-permute-start(f32[2,16,128]{2,1,0:T(8,128)S(1)} %get-tuple-element.27), channel_id=1, source_target_pairs={{32,64},{64,32},{96,128},{128,96},{160,192},{192,160},{224,256},{2... | collective-permute-start | bytes 49160 | tf_op jit(solution)/shard_map/ppermute | solution.py:171
  13.5 0.8 %copy-start.3 = (bf16[16,16,128]{2,1,0:T(8,128)(2,1)S(1)}, bf16[16,16,128]{2,1,0:T(8,128)(2,1)}, u32[]{:S(2)}) copy-start(bf16[16,16,128]{2,1,0:T(8,128)(2,1)} %param.7) | copy-start | bytes 196612
  42.8 3.1 %collective-permute-start.2 = (f32[5,16,128]{2,1,0:T(8,128)S(1)}, f32[5,16,128]{2,1,0:T(8,128)S(1)}, u32[]{:S(2)}, u32[]{:S(2)}) collective-permute-start(f32[5,16,128]{2,1,0:T(8,128)S(1)} %get-tuple-element.39.own_ref), channel_id=1, source_target_pairs={{0,32},{32,0},{64,96},{96,64},{128,160},{160,128},{192,224},{224,1... | collective-permute-start | bytes 122888 | tf_op jit(solution)/shard_map/ppermute | solution.py:301

commit v2 on v1

--- a/solution.py
+++ b/solution.py
@@ -148,7 +148,19 @@
     def rows_y(ref, j):
         return ref[pl.ds(j, nx, stride=ny), :]
 
-    def halves_body(perm_ref, speed_ref, p_ref, half_ref, near_ref, far_ref):
+    def halves_body(
+        p_hbm, source_hbm, por_hbm, perm_hbm, speed_hbm,
+        half_ref, near_ref, far_ref, p_ref, source_ref, por_ref, perm_ref, speed_ref, sems,
+    ):
+        pairs = (
+            (perm_hbm, perm_ref), (speed_hbm, speed_ref), (p_hbm, p_ref),
+            (source_hbm, source_ref), (por_hbm, por_ref),
+        )
+        copies = [pltpu.make_async_copy(a, b, sems.at[n]) for n, (a, b) in enumerate(pairs)]
+        for copy in copies:
+            copy.start()
+        for copy in copies[:3]:
+            copy.wait()
         for i in range(nx):
             root = lax.rsqrt(plane(perm_ref, i, ny).astype(F32))
             half_ref[i * ny : (i + 1) * ny, :] = (0.5 * root) * (
@@ -160,11 +172,30 @@
             high = rows_y(ref, ny - 1)
             near_ref[k] = jnp.where(even, high, low)
             far_ref[k] = jnp.where(even, low, high)
-
-    half, near_send, far_send = call(
-        halves_body, [(cells, nz), (2, nx, nz), (2, nx, nz)], [], permeability, speed, pressure,
+        for copy in copies[3:]:
+            copy.wait()
+
+    vmem = pl.BlockSpec(memory_space=pltpu.VMEM)
+    half, near_send, far_send, pressure, source, porosity = pl.pallas_call(
+        halves_body,
+        out_shape=[
+            jax.ShapeDtypeStruct((cells, nz), F32),
+            jax.ShapeDtypeStruct((2, nx, nz), F32),
+            jax.ShapeDtypeStruct((2, nx, nz), F32),
+            jax.ShapeDtypeStruct((cells, nz), F32),
+            jax.ShapeDtypeStruct((cells, nz), F32),
+            jax.ShapeDtypeStruct((cells, nz), porosity.dtype),
+        ],
+        in_specs=[pl.BlockSpec(memory_space=pltpu.HBM)] * 5,
+        out_specs=[vmem] * 6,
+        scratch_shapes=[
+            pltpu.VMEM((cells, nz), permeability.dtype),
+            pltpu.VMEM((cells, nz), speed.dtype),
+            pltpu.SemaphoreType.DMA((5,)),
+        ],
+        compiler_params=pltpu.CompilerParams(vmem_limit_bytes=16 * 1024 * 1024),
         name="halves",
-    )
+    )(*(pltpu.with_memory_space_constraint(a, pltpu.HBM) for a in (pressure, source, porosity, permeability, speed)))
     far_pairs = []
     for i in range(1, count_gy - 1, 2):
         far_pairs += [(i, i + 1), (i + 1, i)]
@@ -215,7 +246,7 @@
     )
 
     def edges_body(
-        right0_ref, p_ref, half_ref, near_ref, far_ref, xup_ref, xdown_ref, xends_ref, right_ref, send_ref
+        right0_ref, p_ref, half_ref, far_ref, near_ref, xup_ref, xdown_ref, xends_ref, right_ref, send_ref
     ):
         place = lax.axis_index("gy")
         even = lax.rem(place, 2) == 0
@@ -237,7 +268,7 @@
 
     right, near_x = call(
         edges_body, [(cells, nz), (NEAR_X, 5, ny, nz)], [],
-        right0, pressure, half, near_got, far_got, xup, xdown, xends, name="edges",
+        right0, pressure, half, far_got, near_got, xup, xdown, xends, name="edges",
     )
     near_x = lax.all_to_all(near_x, "gx", 0, 0, axis_index_groups=near_x_groups)
 

time: 68.2 us -> 64.4 us (0.944)
  local copies, waits for them, and re-layouts: 3.42 us -> 0 us
  starting transfers between devices: 12.8 us -> 14.9 us
  waiting for transfers between devices: 3.07 us -> 1.28 us
  blocking collectives: 46.9 us -> 45.2 us
  Pallas kernels: 1.58 us -> 2.62 us
    ppermute x1, starting transfers between devices: 8.92 us -> 4.85 us  [local_step(): lax.ppermute(near_send, 'gy', [(i, i ^ 1) for i in range(count_gy)])]
    ppermute x1, starting transfers between devices: 1.92 us -> 5.48 us  [local_step(): lax.ppermute(pair_send, 'gy', [(i, i ^ 1) for i in range(count_gy)])]
    unnamed x12 -> x0, local copies, waits for them, and re-layouts: 3.42 us -> none
    ppermute x1, starting transfers between devices: 1.92 us -> 4.59 us  [local_step(): far_got = lax.ppermute(far_send, 'gy', far_pairs)]
    all_to_all x1, blocking collectives: 21 us -> 18.5 us  [local_step(): lax.all_to_all(far_y_send, 'gy', 0, 0, axis_index_groups=far_y_groups)]
    ppermute x1, waiting for transfers between devices: 1.88 us -> 0.01 us  [local_step(): far_got = lax.ppermute(far_send, 'gy', far_pairs)]
    pallas_call x0 -> x1, Pallas kernels: none -> 1.08 us  [local_step(): pl.pallas_call(halves_body, out_shape=[jax.ShapeDtypeStruct((cells, nz),...]
    all_to_all x1, blocking collectives: 18.5 us -> 19.3 us  [local_step(): lax.all_to_all(far_x_send, 'gx', 0, 0, axis_index_groups=far_x_groups)]
where the time goes in v2:
time: 64.4 us; the launch traced here: 64.1 us
  blocking collectives  45.2 us (70%)
  starting transfers between devices  14.9 us (23%)
  Pallas kernels  2.62 us (4%)
  waiting for transfers between devices  1.28 us (2%)
    all_to_all x1, blocking collectives, local_step(): lax.all_to_all(far_x_send, 'gx', 0, 0, axis_index_groups=far_x_groups)  19.3 us
    all_to_all x1, blocking collectives, local_step(): lax.all_to_all(far_y_send, 'gy', 0, 0, axis_index_groups=far_y_groups)  18.5 us
    all_to_all x1, blocking collectives, local_step(): near_x = lax.all_to_all(near_x, 'gx', 0, 0, axis_index_groups=near_x_groups)  7.46 us
    ppermute x1, starting transfers between devices, local_step(): lax.ppermute(pair_send, 'gy', [(i, i ^ 1) for i in range(count_gy)])  5.48 us
    ppermute x1, starting transfers between devices, local_step(): lax.ppermute(near_send, 'gy', [(i, i ^ 1) for i in range(count_gy)])  4.85 us
    ppermute x1, starting transfers between devices, local_step(): far_got = lax.ppermute(far_send, 'gy', far_pairs)  4.59 us
    pallas_call x6, Pallas kernels, call(): pl.pallas_call(body, out_shape=[jax.ShapeDtypeStruct(s, F32) for s in sha...  1.54 us
  transfers between devices with their start and end apart: 3, of which 2 were waited for; matrix products, arithmetic and copies ran while one was open for 0% of the time, Pallas kernels for 1%

profile of v2, /device:TPU:1, one launch (start us, length us, event | category | flops | bytes accessed | tf_op | source)
XLA Modules:
  0.0 64.1 jit_solution(2707334783408070695)
XLA Ops:
  0.0 1.1 %halves.1 = (f32[256,128]{1,0:T(8,128)S(1)}, f32[2,16,128]{2,1,0:T(8,128)S(1)}, f32[2,16,128]{2,1,0:T(8,128)S(1)}, f32[256,128]{1,0:T(8,128)S(1)}, f32[256,128]{1,0:T(8,128)S(1)}, /*index=5*/bf16[256,128]{1,0:T(8,128)(2,1)S(1)}) custom-call(f32[256,128]{1,0:T(8,128)} %bitcast.6, f32[256,128]{1,0:T(8,128)} %bitcast.7, bf16[256,128]{1,0:T(8,128)(2,1)} %bitcast.8, ...), custom_call_target="tpu_custom_call" | custom-call | tf_op jit(solution)/shard_map/halves/pallas_call | solution.py:179
  1.1 4.6 %collective-permute-start = (f32[2,16,128]{2,1,0:T(8,128)S(1)}, f32[2,16,128]{2,1,0:T(8,128)S(1)}, u32[]{:S(2)}, u32[]{:S(2)}) collective-permute-start(f32[2,16,128]{2,1,0:T(8,128)S(1)} %get-tuple-element.32), channel_id=1, source_target_pairs={{32,64},{64,32},{96,128},{128,96},{160,192},{192,160},{224,256},{2... | collective-permute-start | bytes 49160 | tf_op jit(solution)/shard_map/ppermute | solution.py:202
  5.7 4.9 %collective-permute-start.1 = (f32[2,16,128]{2,1,0:T(8,128)S(1)}, f32[2,16,128]{2,1,0:T(8,128)S(1)}, u32[]{:S(2)}, u32[]{:S(2)}) collective-permute-start(f32[2,16,128]{2,1,0:T(8,128)S(1)} %get-tuple-element.33), channel_id=1, source_target_pairs={{0,32},{32,0},{64,96},{96,64},{128,160},{160,128},{192,224},{224,1... | collective-permute-start | bytes 49160 | tf_op jit(solution)/shard_map/ppermute | solution.py:203
  10.6 0.4 inner.1
  10.9 0.0 collective-permute-done.far_ref
  10.9 0.4 collective-permute-done.1.near_ref
  11.4 0.1 edges.1
  11.5 7.5 %all_to_all.15.got_ref = f32[4,5,16,128]{3,2,1,0:T(8,128)S(1)} all-to-all(f32[4,5,16,128]{3,2,1,0:T(8,128)S(1)} %get-tuple-element.37), channel_id=1, replica_groups={{0,1,2,3},{4,5,6,7},{8,9,10,11},{12,13,14,15},{16,17,18,19},{20,21,22,2..., dimensions={0} | all-to-all | bytes 327680 | tf_op jit(solution)/shard_map/all_to_all | solution.py:273
  19.0 19.3 %all_to_all.16.got_ref = f32[8,5,16,128]{3,2,1,0:T(8,128)S(1)} all-to-all(f32[8,5,16,128]{3,2,1,0:T(8,128)S(1)} %get-tuple-element.38), channel_id=1, replica_groups={{0,4,8,12,16,20,24,28},{1,5,9,13,17,21,25,29},{2,6,10,14,18,22,26,30},{..., dimensions={0} | all-to-all | bytes 655360 | tf_op jit(solution)/shard_map/all_to_all | solution.py:287
  38.2 0.2 along_x.1
  38.4 5.5 %collective-permute-start.2 = (f32[5,16,128]{2,1,0:T(8,128)S(1)}, f32[5,16,128]{2,1,0:T(8,128)S(1)}, u32[]{:S(2)}, u32[]{:S(2)}) collective-permute-start(f32[5,16,128]{2,1,0:T(8,128)S(1)} %get-tuple-element.45.own_ref), channel_id=1, source_target_pairs={{0,32},{32,0},{64,96},{96,64},{128,160},{160,128},{192,224},{224,1... | collective-permute-start | bytes 122888 | tf_op jit(solution)/shard_map/ppermute | solution.py:332
  43.9 0.8 %collective-permute-done.2.got_ref = f32[5,16,128]{2,1,0:T(8,128)S(1)} collective-permute-done((f32[5,16,128]{2,1,0:T(8,128)S(1)}, f32[5,16,128]{2,1,0:T(8,128)S(1)}, u32[]{:S(2)}, u32[]{:S(2)}) %collective-permute-start.2) | collective-permute-done | bytes 40992 | tf_op jit(solution)/shard_map/ppermute | solution.py:332
  44.8 18.5 %all_to_all.17.got_ref = f32[8,5,16,128]{3,2,1,0:T(8,128)S(1)} all-to-all(f32[8,5,16,128]{3,2,1,0:T(8,128)S(1)} %get-tuple-element.46), channel_id=1, replica_groups={{0,64,128,192,256,320,384,448},{32,96,160,224,288,352,416,480},{1,65,12..., dimensions={0} | all-to-all | bytes 655360 | tf_op jit(solution)/shard_map/all_to_all | solution.py:348
  63.3 0.8 %updated.1 = f32[256,128]{1,0:T(8,128)} custom-call(f32[8,5,16,128]{3,2,1,0:T(8,128)S(1)} %all_to_all.17.got_ref, f32[3,16,128]{2,1,0:T(8,128)S(1)} %get-tuple-element.47.tree_ref, f32[16,16,128]{2,1,0:T(8,128)S(1)} %get-tuple-element.48.yright_ref, f32[256,128]{1,0:T(8,128)S(1)} %get-tuple-element.30.half_ref, f32[256,128]{1,0:T(8,128)S(1)} %get-tuple-element.27.p_ref, ...), custom_call_target="tpu_custom_call" | custom-call | tf_op jit(solution)/shard_map/updated/pallas_call | solution.py:138
  (2 shorter events, 0.1 us)
Async XLA Ops:
  1.1 9.8 %collective-permute-start = (f32[2,16,128]{2,1,0:T(8,128)S(1)}, f32[2,16,128]{2,1,0:T(8,128)S(1)}, u32[]{:S(2)}, u32[]{:S(2)}) collective-permute-start(f32[2,16,128]{2,1,0:T(8,128)S(1)} %get-tuple-element.32), channel_id=1, source_target_pairs={{32,64},{64,32},{96,128},{128,96},{160,192},{192,160},{224,256},{2... | collective-permute-start | bytes 49160 | tf_op jit(solution)/shard_map/ppermute | solution.py:202
  5.7 5.7 %collective-permute-start.1 = (f32[2,16,128]{2,1,0:T(8,128)S(1)}, f32[2,16,128]{2,1,0:T(8,128)S(1)}, u32[]{:S(2)}, u32[]{:S(2)}) collective-permute-start(f32[2,16,128]{2,1,0:T(8,128)S(1)} %get-tuple-element.33), channel_id=1, source_target_pairs={{0,32},{32,0},{64,96},{96,64},{128,160},{160,128},{192,224},{224,1... | collective-permute-start | bytes 49160 | tf_op jit(solution)/shard_map/ppermute | solution.py:203
  38.4 6.3 %collective-permute-start.2 = (f32[5,16,128]{2,1,0:T(8,128)S(1)}, f32[5,16,128]{2,1,0:T(8,128)S(1)}, u32[]{:S(2)}, u32[]{:S(2)}) collective-permute-start(f32[5,16,128]{2,1,0:T(8,128)S(1)} %get-tuple-element.45.own_ref), channel_id=1, source_target_pairs={{0,32},{32,0},{64,96},{96,64},{128,160},{160,128},{192,224},{224,1... | collective-permute-start | bytes 122888 | tf_op jit(solution)/shard_map/ppermute | solution.py:332

commit v3 on v2

--- a/solution.py
+++ b/solution.py
@@ -126,6 +126,7 @@
     far_y = count_gy // NEAR_Y
     near_x_groups = [[z * NEAR_X + x for x in range(NEAR_X)] for z in range(far_x)]
     far_x_groups = [[z * NEAR_X + x for z in range(far_x)] for x in range(NEAR_X)]
+    near_y_groups = [[y * NEAR_Y + c for c in range(NEAR_Y)] for y in range(far_y)]
     far_y_groups = [[y * NEAR_Y + c for y in range(far_y)] for c in range(NEAR_Y)]
     cells = nx * ny
     pressure = pressure.reshape(cells, nz)
@@ -200,7 +201,7 @@
     for i in range(1, count_gy - 1, 2):
         far_pairs += [(i, i + 1), (i + 1, i)]
     far_got = lax.ppermute(far_send, "gy", far_pairs)
-    near_got = lax.ppermute(near_send, "gy", [(i, i ^ 1) for i in range(count_gy)])
+    near_got = lax.all_gather(near_send, "gy", axis=0, axis_index_groups=near_y_groups)
 
     def inner_body(
         p_ref, source_ref, por_ref, half_ref,
@@ -252,9 +253,10 @@
         even = lax.rem(place, 2) == 0
         right_ref[...] = right0_ref[...]
         for j, is_end, low in ((0, place == 0, True), (ny - 1, place == count_gy - 1, False)):
-            first, second = (far_ref, near_ref) if low else (near_ref, far_ref)
-            other_h = jnp.where(even, first[0], second[0])
-            other_p = jnp.where(even, first[1], second[1])
+            other_h, other_p = (
+                jnp.where(even, far_ref[k], near_ref[0, k]) if low else jnp.where(even, near_ref[1, k], far_ref[k])
+                for k in range(2)
+            )
             flux = (other_p - rows_y(p_ref, j)) / (other_h + rows_y(half_ref, j))
             flux = jnp.where(is_end, 0.0, flux)
             right_ref[pl.ds(j, nx, stride=ny), :] = rows_y(right_ref, j) + flux
@@ -329,12 +331,10 @@
         far_x_got, x_tree, right, half, ratio, pressure, xup, xends, yup, ydown, yends,
         name="along_x",
     )
-    pair_got = lax.ppermute(pair_send, "gy", [(i, i ^ 1) for i in range(count_gy)])
-
-    def pair_body(own_ref, got_ref, send_ref, tree_ref):
-        even = lax.rem(lax.axis_index("gy"), 2) == 0
-        left = tuple(jnp.where(even, own_ref[k], got_ref[k]) for k in range(5))
-        right = tuple(jnp.where(even, got_ref[k], own_ref[k]) for k in range(5))
+    pair_got = lax.all_gather(pair_send, "gy", axis=0, axis_index_groups=near_y_groups)
+
+    def pair_body(got_ref, send_ref, tree_ref):
+        left, right = (tuple(got_ref[n, k] for k in range(5)) for n in range(NEAR_Y))
         merged, face = join(left, right)
         for k in range(5):
             for target in range(far_y):
@@ -343,7 +343,7 @@
             tree_ref[k] = face[k]
 
     far_y_send, y_tree = call(
-        pair_body, [(far_y, 5, nx, nz), (3, nx, nz)], [], pair_send, pair_got, name="y_pair"
+        pair_body, [(far_y, 5, nx, nz), (3, nx, nz)], [], pair_got, name="y_pair"
     )
     far_y_got = lax.all_to_all(far_y_send, "gy", 0, 0, axis_index_groups=far_y_groups)
 

time: 64.4 us -> 62.8 us (0.975)
  starting transfers between devices: 14.9 us -> 4.59 us
  blocking collectives: 45.2 us -> 55.3 us
  waiting for transfers between devices: 1.28 us -> 0.01 us
    ppermute x2 -> x0, starting transfers between devices: 10.3 us -> none  [the longest x1 5.48 us: local_step(): lax.ppermute(pair_send, 'gy', [(i, i ^ 1) for i in range(count_gy)])]
    all_gather x0 -> x2, blocking collectives: none -> 9.52 us  [the longest x1 5.08 us: local_step(): lax.all_gather(pair_send, 'gy', axis=0, axis_index_groups=near_y_groups)]
    ppermute x2 -> x0, waiting for transfers between devices: 1.28 us -> none  [the longest x1 0.85 us: local_step(): lax.ppermute(pair_send, 'gy', [(i, i ^ 1) for i in range(count_gy)])]
  transfers between devices with their start and end apart: 3 -> 1, of which waited for: 2 -> 0; matrix products, arithmetic and copies ran while one was open for 0% -> 0% of each run, Pallas kernels for 1% -> 1%
where the time goes in v3:
time: 62.8 us; the launch traced here: 62.5 us
  blocking collectives  55.3 us (88%)
  starting transfers between devices  4.59 us (7%)
  Pallas kernels  2.62 us (4%)
    all_to_all x1, blocking collectives, local_step(): lax.all_to_all(far_x_send, 'gx', 0, 0, axis_index_groups=far_x_groups)  19.3 us
    all_to_all x1, blocking collectives, local_step(): lax.all_to_all(far_y_send, 'gy', 0, 0, axis_index_groups=far_y_groups)  19 us
    all_to_all x1, blocking collectives, local_step(): near_x = lax.all_to_all(near_x, 'gx', 0, 0, axis_index_groups=near_x_groups)  7.47 us
    all_gather x1, blocking collectives, local_step(): lax.all_gather(pair_send, 'gy', axis=0, axis_index_groups=near_y_groups)  5.08 us
    ppermute x1, starting transfers between devices, local_step(): far_got = lax.ppermute(far_send, 'gy', far_pairs)  4.59 us
    all_gather x1, blocking collectives, local_step(): lax.all_gather(near_send, 'gy', axis=0, axis_index_groups=near_y_groups)  4.44 us
    pallas_call x6, Pallas kernels, call(): pl.pallas_call(body, out_shape=[jax.ShapeDtypeStruct(s, F32) for s in sha...  1.54 us
  transfers between devices with their start and end apart: 1, of which 0 were waited for; matrix products, arithmetic and copies ran while one was open for 0% of the time, Pallas kernels for 1%

profile of v3, /device:TPU:1, one launch (start us, length us, event | category | flops | bytes accessed | tf_op | source)
XLA Modules:
  0.0 62.5 jit_solution(17468605261202665426)
XLA Ops:
  0.0 1.1 %halves.1 = (f32[256,128]{1,0:T(8,128)S(1)}, f32[2,16,128]{2,1,0:T(8,128)S(1)}, f32[2,16,128]{2,1,0:T(8,128)S(1)}, f32[256,128]{1,0:T(8,128)S(1)}, f32[256,128]{1,0:T(8,128)S(1)}, /*index=5*/bf16[256,128]{1,0:T(8,128)(2,1)S(1)}) custom-call(f32[256,128]{1,0:T(8,128)} %bitcast.10, f32[256,128]{1,0:T(8,128)} %bitcast.11, bf16[256,128]{1,0:T(8,128)(2,1)} %bitcast.12, ...), custom_call_target="tpu_custom_call" | custom-call | tf_op jit(solution)/shard_map/halves/pallas_call | solution.py:180
  1.1 4.6 %collective-permute-start = (f32[2,16,128]{2,1,0:T(8,128)S(1)}, f32[2,16,128]{2,1,0:T(8,128)S(1)}, u32[]{:S(2)}, u32[]{:S(2)}) collective-permute-start(f32[2,16,128]{2,1,0:T(8,128)S(1)} %get-tuple-element.32), channel_id=1, source_target_pairs={{32,64},{64,32},{96,128},{128,96},{160,192},{192,160},{224,256},{2... | collective-permute-start | bytes 49160 | tf_op jit(solution)/shard_map/ppermute | solution.py:203
  5.7 0.4 inner.1
  6.1 4.4 %all-gather = f32[4,16,128]{2,1,0:T(8,128)S(1)} all-gather(f32[2,16,128]{2,1,0:T(8,128)S(1)} %get-tuple-element.33), channel_id=2, replica_groups={{0,32},{64,96},{128,160},{192,224},{256,288},{320,352},{384,416},{448,4..., dimensions={0}, use_global_device_ids=true | all-gather | bytes 49152 | tf_op jit(solution)/shard_map/all_gather | solution.py:204
  10.5 0.0 collective-permute-done.far_ref
  10.5 0.1 edges.1
  10.6 7.5 %all_to_all.15.got_ref = f32[4,5,16,128]{3,2,1,0:T(8,128)S(1)} all-to-all(f32[4,5,16,128]{3,2,1,0:T(8,128)S(1)} %get-tuple-element.37), channel_id=1, replica_groups={{0,1,2,3},{4,5,6,7},{8,9,10,11},{12,13,14,15},{16,17,18,19},{20,21,22,2..., dimensions={0} | all-to-all | bytes 327680 | tf_op jit(solution)/shard_map/all_to_all | solution.py:275
  18.1 19.3 %all_to_all.16.got_ref = f32[8,5,16,128]{3,2,1,0:T(8,128)S(1)} all-to-all(f32[8,5,16,128]{3,2,1,0:T(8,128)S(1)} %get-tuple-element.38), channel_id=1, replica_groups={{0,4,8,12,16,20,24,28},{1,5,9,13,17,21,25,29},{2,6,10,14,18,22,26,30},{..., dimensions={0} | all-to-all | bytes 655360 | tf_op jit(solution)/shard_map/all_to_all | solution.py:289
  37.4 0.2 along_x.1
  37.6 5.1 %all-gather.1 = f32[10,16,128]{2,1,0:T(8,128)S(1)} all-gather(f32[5,16,128]{2,1,0:T(8,128)S(1)} %get-tuple-element.45), channel_id=3, replica_groups={{0,32},{64,96},{128,160},{192,224},{256,288},{320,352},{384,416},{448,4..., dimensions={0}, use_global_device_ids=true | all-gather | bytes 122880 | tf_op jit(solution)/shard_map/all_gather | solution.py:334
  42.7 19.0 %all_to_all.17.got_ref = f32[8,5,16,128]{3,2,1,0:T(8,128)S(1)} all-to-all(f32[8,5,16,128]{3,2,1,0:T(8,128)S(1)} %get-tuple-element.46), channel_id=1, replica_groups={{0,64,128,192,256,320,384,448},{32,96,160,224,288,352,416,480},{1,65,12..., dimensions={0} | all-to-all | bytes 655360 | tf_op jit(solution)/shard_map/all_to_all | solution.py:348
  61.7 0.8 %updated.1 = f32[256,128]{1,0:T(8,128)} custom-call(f32[8,5,16,128]{3,2,1,0:T(8,128)S(1)} %all_to_all.17.got_ref, f32[3,16,128]{2,1,0:T(8,128)S(1)} %get-tuple-element.47.tree_ref, f32[16,16,128]{2,1,0:T(8,128)S(1)} %get-tuple-element.48.yright_ref, f32[256,128]{1,0:T(8,128)S(1)} %get-tuple-element.30.half_ref, f32[256,128]{1,0:T(8,128)S(1)} %get-tuple-element.27.p_ref, ...), custom_call_target="tpu_custom_call" | custom-call | tf_op jit(solution)/shard_map/updated/pallas_call | solution.py:139
  (2 shorter events, 0.1 us)
Async XLA Ops:
  1.1 9.4 %collective-permute-start = (f32[2,16,128]{2,1,0:T(8,128)S(1)}, f32[2,16,128]{2,1,0:T(8,128)S(1)}, u32[]{:S(2)}, u32[]{:S(2)}) collective-permute-start(f32[2,16,128]{2,1,0:T(8,128)S(1)} %get-tuple-element.32), channel_id=1, source_target_pairs={{32,64},{64,32},{96,128},{128,96},{160,192},{192,160},{224,256},{2... | collective-permute-start | bytes 49160 | tf_op jit(solution)/shard_map/ppermute | solution.py:203

commit v4 on v3

--- a/solution.py
+++ b/solution.py
@@ -7,8 +7,8 @@
 
 FORCH = 0.55
 STEP = 500.0
-NEAR_X = 4
-NEAR_Y = 2
+NEAR_X = 8
+NEAR_Y = 4
 F32 = jnp.float32
 
 
@@ -127,6 +127,7 @@
     near_x_groups = [[z * NEAR_X + x for x in range(NEAR_X)] for z in range(far_x)]
     far_x_groups = [[z * NEAR_X + x for z in range(far_x)] for x in range(NEAR_X)]
     near_y_groups = [[y * NEAR_Y + c for c in range(NEAR_Y)] for y in range(far_y)]
+    chip_groups = [[y, y + 1] for y in range(0, count_gy, 2)]
     far_y_groups = [[y * NEAR_Y + c for y in range(far_y)] for c in range(NEAR_Y)]
     cells = nx * ny
     pressure = pressure.reshape(cells, nz)
@@ -201,7 +202,7 @@
     for i in range(1, count_gy - 1, 2):
         far_pairs += [(i, i + 1), (i + 1, i)]
     far_got = lax.ppermute(far_send, "gy", far_pairs)
-    near_got = lax.all_gather(near_send, "gy", axis=0, axis_index_groups=near_y_groups)
+    near_got = lax.all_gather(near_send, "gy", axis=0, axis_index_groups=chip_groups)
 
     def inner_body(
         p_ref, source_ref, por_ref, half_ref,
@@ -334,16 +335,16 @@
     pair_got = lax.all_gather(pair_send, "gy", axis=0, axis_index_groups=near_y_groups)
 
     def pair_body(got_ref, send_ref, tree_ref):
-        left, right = (tuple(got_ref[n, k] for k in range(5)) for n in range(NEAR_Y))
-        merged, face = join(left, right)
+        pieces = [tuple(got_ref[n, k] for k in range(5)) for n in range(NEAR_Y)]
+        merged, tree = join_all(pieces)
         for k in range(5):
             for target in range(far_y):
                 send_ref[target, k] = merged[k]
-        for k in range(3):
-            tree_ref[k] = face[k]
+        for k, value in enumerate(tree_values(tree)):
+            tree_ref[k] = value
 
     far_y_send, y_tree = call(
-        pair_body, [(far_y, 5, nx, nz), (3, nx, nz)], [], pair_got, name="y_pair"
+        pair_body, [(far_y, 5, nx, nz), (3 * (NEAR_Y - 1), nx, nz)], [], pair_got, name="y_pair"
     )
     far_y_got = lax.all_to_all(far_y_send, "gy", 0, 0, axis_index_groups=far_y_groups)
 
@@ -360,7 +361,7 @@
             far_faces[k] = zero if value is None else value
         low = far_faces[far]
         high = far_faces[far + 1]
-        tree = tree_of(tree_shape(NEAR_Y), [tree_ref[k] for k in range(3)])
+        tree = tree_of(tree_shape(NEAR_Y), [tree_ref[k] for k in range(3 * (NEAR_Y - 1))])
         for k, value in enumerate(face_fluxes(tree, low, high)):
             near_faces[k] = value
         low = near_faces[near]

time: 62.8 us -> 61.4 us (0.978)
  blocking collectives: 55.3 us -> 53.9 us
    all_to_all x1, blocking collectives: 19 us -> 13.7 us  [local_step(): lax.all_to_all(far_y_send, 'gy', 0, 0, axis_index_groups=far_y_groups)]
    all_gather x1, blocking collectives: 5.08 us -> 8.87 us  [local_step(): lax.all_gather(pair_send, 'gy', axis=0, axis_index_groups=near_y_groups)]
    all_to_all x1, blocking collectives: 7.47 us -> 10.6 us  [local_step(): near_x = lax.all_to_all(near_x, 'gx', 0, 0, axis_index_groups=near_x_groups)]
    all_to_all x1, blocking collectives: 19.3 us -> 16.3 us  [local_step(): lax.all_to_all(far_x_send, 'gx', 0, 0, axis_index_groups=far_x_groups)]
where the time goes in v4:
time: 61.4 us; the launch traced here: 61.2 us
  blocking collectives  53.9 us (88%)
  starting transfers between devices  4.59 us (7%)
  Pallas kernels  2.61 us (4%)
    all_to_all x1, blocking collectives, local_step(): lax.all_to_all(far_x_send, 'gx', 0, 0, axis_index_groups=far_x_groups)  16.3 us
    all_to_all x1, blocking collectives, local_step(): lax.all_to_all(far_y_send, 'gy', 0, 0, axis_index_groups=far_y_groups)  13.7 us
    all_to_all x1, blocking collectives, local_step(): near_x = lax.all_to_all(near_x, 'gx', 0, 0, axis_index_groups=near_x_groups)  10.6 us
    all_gather x1, blocking collectives, local_step(): lax.all_gather(pair_send, 'gy', axis=0, axis_index_groups=near_y_groups)  8.87 us
    ppermute x1, starting transfers between devices, local_step(): far_got = lax.ppermute(far_send, 'gy', far_pairs)  4.59 us
    all_gather x1, blocking collectives, local_step(): lax.all_gather(near_send, 'gy', axis=0, axis_index_groups=chip_groups)  4.44 us
    pallas_call x6, Pallas kernels, call(): pl.pallas_call(body, out_shape=[jax.ShapeDtypeStruct(s, F32) for s in sha...  1.53 us
  transfers between devices with their start and end apart: 1, of which 0 were waited for; matrix products, arithmetic and copies ran while one was open for 0% of the time, Pallas kernels for 1%

profile of v4, /device:TPU:1, one launch (start us, length us, event | category | flops | bytes accessed | tf_op | source)
XLA Modules:
  0.0 61.2 jit_solution(15091265192712564509)
XLA Ops:
  0.0 1.1 %halves.1 = (f32[256,128]{1,0:T(8,128)S(1)}, f32[2,16,128]{2,1,0:T(8,128)S(1)}, f32[2,16,128]{2,1,0:T(8,128)S(1)}, f32[256,128]{1,0:T(8,128)S(1)}, f32[256,128]{1,0:T(8,128)S(1)}, /*index=5*/bf16[256,128]{1,0:T(8,128)(2,1)S(1)}) custom-call(f32[256,128]{1,0:T(8,128)} %bitcast.10, f32[256,128]{1,0:T(8,128)} %bitcast.11, bf16[256,128]{1,0:T(8,128)(2,1)} %bitcast.12, ...), custom_call_target="tpu_custom_call" | custom-call | tf_op jit(solution)/shard_map/halves/pallas_call | solution.py:181
  1.1 4.6 %collective-permute-start = (f32[2,16,128]{2,1,0:T(8,128)S(1)}, f32[2,16,128]{2,1,0:T(8,128)S(1)}, u32[]{:S(2)}, u32[]{:S(2)}) collective-permute-start(f32[2,16,128]{2,1,0:T(8,128)S(1)} %get-tuple-element.32), channel_id=1, source_target_pairs={{32,64},{64,32},{96,128},{128,96},{160,192},{192,160},{224,256},{2... | collective-permute-start | bytes 49160 | tf_op jit(solution)/shard_map/ppermute | solution.py:204
  5.7 0.4 inner.1
  6.1 4.4 %all-gather = f32[4,16,128]{2,1,0:T(8,128)S(1)} all-gather(f32[2,16,128]{2,1,0:T(8,128)S(1)} %get-tuple-element.33), channel_id=2, replica_groups={{0,32},{64,96},{128,160},{192,224},{256,288},{320,352},{384,416},{448,4..., dimensions={0}, use_global_device_ids=true | all-gather | bytes 49152 | tf_op jit(solution)/shard_map/all_gather | solution.py:205
  10.5 0.0 collective-permute-done.far_ref
  10.5 0.1 edges.1
  10.6 10.6 %all_to_all.15.got_ref = f32[8,5,16,128]{3,2,1,0:T(8,128)S(1)} all-to-all(f32[8,5,16,128]{3,2,1,0:T(8,128)S(1)} %get-tuple-element.37), channel_id=1, replica_groups={{0,1,2,3,4,5,6,7},{8,9,10,11,12,13,14,15},{16,17,18,19,20,21,22,23},{24..., dimensions={0} | all-to-all | bytes 655360 | tf_op jit(solution)/shard_map/all_to_all | solution.py:276
  21.2 16.3 %all_to_all.16.got_ref = f32[4,5,16,128]{3,2,1,0:T(8,128)S(1)} all-to-all(f32[4,5,16,128]{3,2,1,0:T(8,128)S(1)} %get-tuple-element.38), channel_id=1, replica_groups={{0,8,16,24},{1,9,17,25},{2,10,18,26},{3,11,19,27},{4,12,20,28},{5,13,21..., dimensions={0} | all-to-all | bytes 327680 | tf_op jit(solution)/shard_map/all_to_all | solution.py:290
  37.6 0.2 along_x.1
  37.8 8.9 %all-gather.1 = f32[20,16,128]{2,1,0:T(8,128)S(1)} all-gather(f32[5,16,128]{2,1,0:T(8,128)S(1)} %get-tuple-element.45), channel_id=3, replica_groups={{0,32,64,96},{128,160,192,224},{256,288,320,352},{384,416,448,480},{1,3..., dimensions={0}, use_global_device_ids=true | all-gather | bytes 204800 | tf_op jit(solution)/shard_map/all_gather | solution.py:335
  46.7 13.7 %all_to_all.17.got_ref = f32[4,5,16,128]{3,2,1,0:T(8,128)S(1)} all-to-all(f32[4,5,16,128]{3,2,1,0:T(8,128)S(1)} %get-tuple-element.46), channel_id=1, replica_groups={{0,128,256,384},{32,160,288,416},{64,192,320,448},{96,224,352,480},{1,1..., dimensions={0} | all-to-all | bytes 327680 | tf_op jit(solution)/shard_map/all_to_all | solution.py:349
  60.3 0.8 %updated.1 = f32[256,128]{1,0:T(8,128)} custom-call(f32[4,5,16,128]{3,2,1,0:T(8,128)S(1)} %all_to_all.17.got_ref, f32[9,16,128]{2,1,0:T(8,128)S(1)} %get-tuple-element.47.tree_ref, f32[16,16,128]{2,1,0:T(8,128)S(1)} %get-tuple-element.48.yright_ref, f32[256,128]{1,0:T(8,128)S(1)} %get-tuple-element.30.half_ref, f32[256,128]{1,0:T(8,128)S(1)} %get-tuple-element.27.p_ref, ...), custom_call_target="tpu_custom_call" | custom-call | tf_op jit(solution)/shard_map/updated/pallas_call | solution.py:140
  (2 shorter events, 0.1 us)
Async XLA Ops:
  1.1 9.4 %collective-permute-start = (f32[2,16,128]{2,1,0:T(8,128)S(1)}, f32[2,16,128]{2,1,0:T(8,128)S(1)}, u32[]{:S(2)}, u32[]{:S(2)}) collective-permute-start(f32[2,16,128]{2,1,0:T(8,128)S(1)} %get-tuple-element.32), channel_id=1, source_target_pairs={{32,64},{64,32},{96,128},{128,96},{160,192},{192,160},{224,256},{2... | collective-permute-start | bytes 49160 | tf_op jit(solution)/shard_map/ppermute | solution.py:204

commit v5 on v4

--- a/solution.py
+++ b/solution.py
@@ -7,8 +7,11 @@
 
 FORCH = 0.55
 STEP = 500.0
-NEAR_X = 8
-NEAR_Y = 4
+RING_X = 4
+CORES = 2
+NEAR_X = 2 * RING_X
+NEAR_Y = 2 * CORES
+PICKS = ((0, 0, 1, 1), (1, 1, 0, 0))
 F32 = jnp.float32
 
 
@@ -125,10 +128,14 @@
     far_x = count_gx // NEAR_X
     far_y = count_gy // NEAR_Y
     near_x_groups = [[z * NEAR_X + x for x in range(NEAR_X)] for z in range(far_x)]
-    far_x_groups = [[z * NEAR_X + x for z in range(far_x)] for x in range(NEAR_X)]
+    far_x_groups = [
+        [k * NEAR_X + pick[k] * RING_X + x for k in range(far_x)] for pick in PICKS for x in range(RING_X)
+    ]
     near_y_groups = [[y * NEAR_Y + c for c in range(NEAR_Y)] for y in range(far_y)]
-    chip_groups = [[y, y + 1] for y in range(0, count_gy, 2)]
-    far_y_groups = [[y * NEAR_Y + c for y in range(far_y)] for c in range(NEAR_Y)]
+    chip_groups = [[y + c for c in range(CORES)] for y in range(0, count_gy, CORES)]
+    far_y_groups = [
+        [k * NEAR_Y + pick[k] * CORES + c for k in range(far_y)] for pick in PICKS for c in range(CORES)
+    ]
     cells = nx * ny
     pressure = pressure.reshape(cells, nz)
     source = source.reshape(cells, nz)

time: 61.4 us -> 58.7 us (0.956)
  the two profiles are of different devices: /device:TPU:1 before, /device:TPU:8 now
where the time goes in v5:
time: 58.7 us; the launch traced here: 58.5 us
  blocking collectives  53.9 us (92%)
  Pallas kernels  2.61 us (4%)
  starting transfers between devices  1.92 us (3%)
    all_to_all x1, blocking collectives, local_step(): lax.all_to_all(far_x_send, 'gx', 0, 0, axis_index_groups=far_x_groups)  16.5 us
    all_to_all x1, blocking collectives, local_step(): near_x = lax.all_to_all(near_x, 'gx', 0, 0, axis_index_groups=near_x_groups)  14.5 us
    all_to_all x1, blocking collectives, local_step(): lax.all_to_all(far_y_send, 'gy', 0, 0, axis_index_groups=far_y_groups)  14.2 us
    all_gather x1, blocking collectives, local_step(): lax.all_gather(pair_send, 'gy', axis=0, axis_index_groups=near_y_groups)  5.52 us
    all_gather x1, blocking collectives, local_step(): lax.all_gather(near_send, 'gy', axis=0, axis_index_groups=chip_groups)  3.17 us
    ppermute x1, starting transfers between devices, local_step(): far_got = lax.ppermute(far_send, 'gy', far_pairs)  1.92 us
    pallas_call x6, Pallas kernels, call(): pl.pallas_call(body, out_shape=[jax.ShapeDtypeStruct(s, F32) for s in sha...  1.52 us
  transfers between devices with their start and end apart: 1, of which 0 were waited for; matrix products, arithmetic and copies ran while one was open for 0% of the time, Pallas kernels for 1%

profile of v5, /device:TPU:8, one launch (start us, length us, event | category | flops | bytes accessed | tf_op | source)
XLA Modules:
  0.0 58.5 jit_solution(11805151071192919290)
XLA Ops:
  0.0 1.1 %halves.1 = (f32[256,128]{1,0:T(8,128)S(1)}, f32[2,16,128]{2,1,0:T(8,128)S(1)}, f32[2,16,128]{2,1,0:T(8,128)S(1)}, f32[256,128]{1,0:T(8,128)S(1)}, f32[256,128]{1,0:T(8,128)S(1)}, /*index=5*/bf16[256,128]{1,0:T(8,128)(2,1)S(1)}) custom-call(f32[256,128]{1,0:T(8,128)} %bitcast.10, f32[256,128]{1,0:T(8,128)} %bitcast.11, bf16[256,128]{1,0:T(8,128)(2,1)} %bitcast.12, ...), custom_call_target="tpu_custom_call" | custom-call | tf_op jit(solution)/shard_map/halves/pallas_call | solution.py:188
  1.1 1.9 %collective-permute-start = (f32[2,16,128]{2,1,0:T(8,128)S(1)}, f32[2,16,128]{2,1,0:T(8,128)S(1)}, u32[]{:S(2)}, u32[]{:S(2)}) collective-permute-start(f32[2,16,128]{2,1,0:T(8,128)S(1)} %get-tuple-element.32), channel_id=1, source_target_pairs={{32,64},{64,32},{96,128},{128,96},{160,192},{192,160},{224,256},{2... | collective-permute-start | bytes 49160 | tf_op jit(solution)/shard_map/ppermute | solution.py:211
  3.0 0.4 inner.1
  3.4 3.2 %all-gather = f32[4,16,128]{2,1,0:T(8,128)S(1)} all-gather(f32[2,16,128]{2,1,0:T(8,128)S(1)} %get-tuple-element.33), channel_id=2, replica_groups={{0,32},{64,96},{128,160},{192,224},{256,288},{320,352},{384,416},{448,4..., dimensions={0}, use_global_device_ids=true | all-gather | bytes 49152 | tf_op jit(solution)/shard_map/all_gather | solution.py:212
  6.6 0.0 collective-permute-done.far_ref
  6.6 0.1 edges.1
  6.7 14.5 %all_to_all.15.got_ref = f32[8,5,16,128]{3,2,1,0:T(8,128)S(1)} all-to-all(f32[8,5,16,128]{3,2,1,0:T(8,128)S(1)} %get-tuple-element.37), channel_id=1, replica_groups={{0,1,2,3,4,5,6,7},{8,9,10,11,12,13,14,15},{16,17,18,19,20,21,22,23},{24..., dimensions={0} | all-to-all | bytes 655360 | tf_op jit(solution)/shard_map/all_to_all | solution.py:283
  21.2 16.5 %all_to_all.16.got_ref = f32[4,5,16,128]{3,2,1,0:T(8,128)S(1)} all-to-all(f32[4,5,16,128]{3,2,1,0:T(8,128)S(1)} %get-tuple-element.38), channel_id=1, replica_groups={{0,8,20,28},{1,9,21,29},{2,10,22,30},{3,11,23,31},{4,12,16,24},{5,13,17..., dimensions={0} | all-to-all | bytes 327680 | tf_op jit(solution)/shard_map/all_to_all | solution.py:297
  37.7 0.2 along_x.1
  37.9 5.5 %all-gather.1 = f32[20,16,128]{2,1,0:T(8,128)S(1)} all-gather(f32[5,16,128]{2,1,0:T(8,128)S(1)} %get-tuple-element.45), channel_id=3, replica_groups={{0,32,64,96},{128,160,192,224},{256,288,320,352},{384,416,448,480},{1,3..., dimensions={0}, use_global_device_ids=true | all-gather | bytes 204800 | tf_op jit(solution)/shard_map/all_gather | solution.py:342
  43.5 14.2 %all_to_all.17.got_ref = f32[4,5,16,128]{3,2,1,0:T(8,128)S(1)} all-to-all(f32[4,5,16,128]{3,2,1,0:T(8,128)S(1)} %get-tuple-element.46), channel_id=1, replica_groups={{0,128,320,448},{32,160,352,480},{64,192,256,384},{96,224,288,416},{1,1..., dimensions={0} | all-to-all | bytes 327680 | tf_op jit(solution)/shard_map/all_to_all | solution.py:356
  57.7 0.8 %updated.1 = f32[256,128]{1,0:T(8,128)} custom-call(f32[4,5,16,128]{3,2,1,0:T(8,128)S(1)} %all_to_all.17.got_ref, f32[9,16,128]{2,1,0:T(8,128)S(1)} %get-tuple-element.47.tree_ref, f32[16,16,128]{2,1,0:T(8,128)S(1)} %get-tuple-element.48.yright_ref, f32[256,128]{1,0:T(8,128)S(1)} %get-tuple-element.30.half_ref, f32[256,128]{1,0:T(8,128)S(1)} %get-tuple-element.27.p_ref, ...), custom_call_target="tpu_custom_call" | custom-call | tf_op jit(solution)/shard_map/updated/pallas_call | solution.py:147
  (2 shorter events, 0.1 us)
Async XLA Ops:
  1.1 5.5 %collective-permute-start = (f32[2,16,128]{2,1,0:T(8,128)S(1)}, f32[2,16,128]{2,1,0:T(8,128)S(1)}, u32[]{:S(2)}, u32[]{:S(2)}) collective-permute-start(f32[2,16,128]{2,1,0:T(8,128)S(1)} %get-tuple-element.32), channel_id=1, source_target_pairs={{32,64},{64,32},{96,128},{128,96},{160,192},{192,160},{224,256},{2... | collective-permute-start | bytes 49160 | tf_op jit(solution)/shard_map/ppermute | solution.py:211

commit v6 on v5

--- a/solution.py
+++ b/solution.py
@@ -78,47 +78,55 @@
     return ref[i * rows : (i + 1) * rows, :]
 
 
-def eliminate(ratio, half, count):
-    gaps = [half[i] + half[i + 1] for i in range(count - 1)]
-    up = []
-    total = ratio[0]
+def elimination(ratio, half, count, keep):
+    gaps = [half(i) + half(i + 1) for i in range(count - 1)]
+    rising = ratio(0)
+    falling = ratio(count - 1)
+    through = None
     for i in range(count - 1):
-        carry = 1.0 / (1.0 + total * gaps[i])
-        up.append(carry)
-        total = ratio[i + 1] + total * carry
-    last_inv = 1.0 / total
-    down = [None] * (count - 1)
-    total = ratio[count - 1]
-    for i in range(count - 2, -1, -1):
-        carry = 1.0 / (1.0 + total * gaps[i])
-        down[i] = carry
-        total = ratio[i] + total * carry
-    first_inv = 1.0 / total
-    across = last_inv
-    for i in range(count - 2, -1, -1):
-        across = across * up[i]
-    ends = [first_inv + half[0], across, last_inv + half[count - 1], first_inv, last_inv]
-    return gaps, up, down, ends
+        up = 1.0 / (1.0 + rising * gaps[i])
+        rising = ratio(i + 1) + rising * up
+        through = up if through is None else through * up
+        k = count - 2 - i
+        down = 1.0 / (1.0 + falling * gaps[k])
+        falling = ratio(k) + falling * down
+        keep(i, up, through, k, down)
+        yield None
+    last_inv = 1.0 / rising
+    first_inv = 1.0 / falling
+    yield (first_inv + half(0), through * last_inv, last_inv + half(count - 1), first_inv, last_inv)
+
+
+def interleave(*parts):
+    last = [None] * len(parts)
+    running = list(range(len(parts)))
+    while running:
+        for n in list(running):
+            try:
+                last[n] = next(parts[n])
+            except StopIteration:
+                running.remove(n)
+    return last
 
 
 def offsets(right, up, down, first_inv, last_inv, count):
     rising = right[0]
+    falling = right[count - 1]
+    sums = [rising]
     for i in range(count - 1):
         rising = right[i + 1] + up[i] * rising
-    falling = right[count - 1]
+        sums.append(rising)
+        k = count - 2 - i
+        falling = right[k] + down[k] * falling
+    return falling * first_inv, rising * last_inv, sums
+
+
+def substitute(sums, through, gaps, up, last_inv, low, high, count):
+    values = [None] * count
+    values[count - 1] = ((sums[count - 1] + through[count - 2] * low) - high) * last_inv
     for i in range(count - 2, -1, -1):
-        falling = right[i] + down[i] * falling
-    return falling * first_inv, rising * last_inv
-
-
-def substitute(right, gaps, up, last_inv, low, high, count):
-    sums = [right[0] + low]
-    for i in range(count - 1):
-        sums.append(right[i + 1] + up[i] * sums[i])
-    values = [None] * count
-    values[count - 1] = (sums[count - 1] - high) * last_inv
-    for i in range(count - 2, -1, -1):
-        values[i] = up[i] * (values[i + 1] + gaps[i] * sums[i])
+        inner = low if i == 0 else through[i - 1] * low
+        values[i] = up[i] * (values[i + 1] + gaps[i] * (sums[i] + inner))
     return values
 
 
@@ -213,49 +221,56 @@
 
     def inner_body(
         p_ref, source_ref, por_ref, half_ref,
-        right_ref, ratio_ref, xup_ref, xdown_ref, xends_ref, yup_ref, ydown_ref, yends_ref,
+        right_ref, ratio_ref, xup_ref, xthrough_ref, xdown_ref, xends_ref,
+        yup_ref, ythrough_ref, ydown_ref, yends_ref,
     ):
         lane = lax.broadcasted_iota(jnp.int32, (ny, nz), 1)
         row = lax.broadcasted_iota(jnp.int32, (ny, nz), 0)
         for i in range(nx):
-            p = plane(p_ref, i, ny)
-            h = plane(half_ref, i, ny)
-            ratio = plane(por_ref, i, ny).astype(F32) * (1.0 / STEP)
-            ratio_ref[i * ny : (i + 1) * ny, :] = ratio
-            flux_z = (pltpu.roll(p, nz - 1, 1) - p) / (pltpu.roll(h, nz - 1, 1) + h)
-            flux_z = jnp.where(lane == nz - 1, 0.0, flux_z)
-            flux_y = (pltpu.roll(p, ny - 1, 0) - p) / (pltpu.roll(h, ny - 1, 0) + h)
-            flux_y = jnp.where(row == ny - 1, 0.0, flux_y)
-            lap = (flux_z - pltpu.roll(flux_z, 1, 1)) + (flux_y - pltpu.roll(flux_y, 1, 0))
-            right_ref[i * ny : (i + 1) * ny, :] = (lap - plane(source_ref, i, ny)) + ratio * p
-        ratios = [plane(ratio_ref, i, ny) for i in range(nx)]
-        halves = [plane(half_ref, i, ny) for i in range(nx)]
-        _, up, down, ends = eliminate(ratios, halves, nx)
-        for i in range(nx - 1):
-            xup_ref[i] = up[i]
-            xdown_ref[i] = down[i]
+            ratio_ref[i * ny : (i + 1) * ny, :] = plane(por_ref, i, ny).astype(F32) * (1.0 / STEP)
+
+        def right_side():
+            for i in range(nx):
+                p = plane(p_ref, i, ny)
+                h = plane(half_ref, i, ny)
+                flux_z = (pltpu.roll(p, nz - 1, 1) - p) / (pltpu.roll(h, nz - 1, 1) + h)
+                flux_z = jnp.where(lane == nz - 1, 0.0, flux_z)
+                flux_y = (pltpu.roll(p, ny - 1, 0) - p) / (pltpu.roll(h, ny - 1, 0) + h)
+                flux_y = jnp.where(row == ny - 1, 0.0, flux_y)
+                lap = (flux_z - pltpu.roll(flux_z, 1, 1)) + (flux_y - pltpu.roll(flux_y, 1, 0))
+                right_ref[i * ny : (i + 1) * ny, :] = (lap - plane(source_ref, i, ny)) + plane(ratio_ref, i, ny) * p
+                yield None
+
+        def keep_x(i, up, through, k, down):
+            xup_ref[i] = up
+            xthrough_ref[i] = through
+            xdown_ref[k] = down
+
+        def keep_y(i, up, through, k, down):
+            yup_ref[i] = up
+            ythrough_ref[i] = through
+            ydown_ref[k] = down
+
+        xends, yends, _ = interleave(
+            elimination(lambda i: plane(ratio_ref, i, ny), lambda i: plane(half_ref, i, ny), nx, keep_x),
+            elimination(lambda j: rows_y(ratio_ref, j), lambda j: rows_y(half_ref, j), ny, keep_y),
+            right_side(),
+        )
         for k in range(5):
-            xends_ref[k] = ends[k]
-        ratios = [rows_y(ratio_ref, j) for j in range(ny)]
-        halves = [rows_y(half_ref, j) for j in range(ny)]
-        _, up, down, ends = eliminate(ratios, halves, ny)
-        for j in range(ny - 1):
-            yup_ref[j] = up[j]
-            ydown_ref[j] = down[j]
-        for k in range(5):
-            yends_ref[k] = ends[k]
-
-    right0, ratio, xup, xdown, xends, yup, ydown, yends = call(
+            xends_ref[k] = xends[k]
+            yends_ref[k] = yends[k]
+
+    right0, ratio, xup, xthrough, xdown, xends, yup, ythrough, ydown, yends = call(
         inner_body,
         [
-            (cells, nz), (cells, nz), (nx - 1, ny, nz), (nx - 1, ny, nz), (5, ny, nz),
-            (ny - 1, nx, nz), (ny - 1, nx, nz), (5, nx, nz),
+            (cells, nz), (cells, nz), (nx - 1, ny, nz), (nx - 1, ny, nz), (nx - 1, ny, nz), (5, ny, nz),
+            (ny - 1, nx, nz), (ny - 1, nx, nz), (ny - 1, nx, nz), (5, nx, nz),
         ],
         [], pressure, source, porosity, half, name="inner",
     )
 
     def edges_body(
-        right0_ref, p_ref, half_ref, far_ref, near_ref, xup_ref, xdown_ref, xends_ref, right_ref, send_ref
+        right0_ref, p_ref, half_ref, far_ref, near_ref, xup_ref, xdown_ref, xends_ref, sums_ref, send_ref, right_ref
     ):
         place = lax.axis_index("gy")
         even = lax.rem(place, 2) == 0
@@ -271,13 +286,15 @@
         right = [plane(right_ref, i, ny) for i in range(nx)]
         up = [xup_ref[i] for i in range(nx - 1)]
         down = [xdown_ref[i] for i in range(nx - 1)]
-        first, last = offsets(right, up, down, xends_ref[3], xends_ref[4], nx)
+        first, last, sums = offsets(right, up, down, xends_ref[3], xends_ref[4], nx)
+        for i in range(nx):
+            sums_ref[i] = sums[i]
         for k, value in enumerate((xends_ref[0], xends_ref[1], xends_ref[2], first, last)):
             for target in range(NEAR_X):
                 send_ref[target, k] = value
 
-    right, near_x = call(
-        edges_body, [(cells, nz), (NEAR_X, 5, ny, nz)], [],
+    xsums, near_x = call(
+        edges_body, [(nx, ny, nz), (NEAR_X, 5, ny, nz)], [(cells, nz)],
         right0, pressure, half, far_got, near_got, xup, xdown, xends, name="edges",
     )
     near_x = lax.all_to_all(near_x, "gx", 0, 0, axis_index_groups=near_x_groups)
@@ -297,9 +314,9 @@
     far_x_got = lax.all_to_all(far_x_send, "gx", 0, 0, axis_index_groups=far_x_groups)
 
     def along_x_body(
-        got_ref, tree_ref, right_ref, half_ref, ratio_ref, p_ref, xup_ref, xends_ref,
+        got_ref, tree_ref, xsums_ref, half_ref, ratio_ref, p_ref, xup_ref, xthrough_ref, xends_ref,
         yup_ref, ydown_ref, yends_ref,
-        send_ref, yright_ref, far_faces, near_faces, solved_ref,
+        send_ref, ysums_ref, far_faces, near_faces, solved_ref,
     ):
         place = lax.axis_index("gx")
         far = place // NEAR_X
@@ -319,24 +336,25 @@
         high = near_faces[near + 1]
         gaps = [plane(half_ref, i, ny) + plane(half_ref, i + 1, ny) for i in range(nx - 1)]
         up = [xup_ref[i] for i in range(nx - 1)]
-        right = [plane(right_ref, i, ny) for i in range(nx)]
-        values = substitute(right, gaps, up, xends_ref[4], low, high, nx)
+        through = [xthrough_ref[i] for i in range(nx - 1)]
+        sums = [xsums_ref[i] for i in range(nx)]
+        values = substitute(sums, through, gaps, up, xends_ref[4], low, high, nx)
         for i in range(nx):
             solved_ref[i * ny : (i + 1) * ny, :] = plane(ratio_ref, i, ny) * (values[i] - plane(p_ref, i, ny))
         yright = [rows_y(solved_ref, j) for j in range(ny)]
-        for j in range(ny):
-            yright_ref[j] = yright[j]
         up = [yup_ref[j] for j in range(ny - 1)]
         down = [ydown_ref[j] for j in range(ny - 1)]
-        first, last = offsets(yright, up, down, yends_ref[3], yends_ref[4], ny)
+        first, last, sums = offsets(yright, up, down, yends_ref[3], yends_ref[4], ny)
+        for j in range(ny):
+            ysums_ref[j] = sums[j]
         for k, value in enumerate((yends_ref[0], yends_ref[1], yends_ref[2], first, last)):
             send_ref[k] = value
 
-    pair_send, yright = call(
+    pair_send, ysums = call(
         along_x_body,
         [(5, nx, nz), (ny, nx, nz)],
         [(far_x + 1, ny, nz), (NEAR_X + 1, ny, nz), (cells, nz)],
-        far_x_got, x_tree, right, half, ratio, pressure, xup, xends, yup, ydown, yends,
+        far_x_got, x_tree, xsums, half, ratio, pressure, xup, xthrough, xends, yup, ydown, yends,
         name="along_x",
     )
     pair_got = lax.all_gather(pair_send, "gy", axis=0, axis_index_groups=near_y_groups)
@@ -356,7 +374,7 @@
     far_y_got = lax.all_to_all(far_y_send, "gy", 0, 0, axis_index_groups=far_y_groups)
 
     def updated_body(
-        got_ref, tree_ref, yright_ref, half_ref, p_ref, yup_ref, yends_ref, out_ref, far_faces, near_faces
+        got_ref, tree_ref, ysums_ref, half_ref, p_ref, yup_ref, ythrough_ref, yends_ref, out_ref, far_faces, near_faces
     ):
         place = lax.axis_index("gy")
         far = place // NEAR_Y
@@ -376,8 +394,9 @@
         halves = [rows_y(half_ref, j) for j in range(ny)]
         gaps = [halves[j] + halves[j + 1] for j in range(ny - 1)]
         up = [yup_ref[j] for j in range(ny - 1)]
-        right = [yright_ref[j] for j in range(ny)]
-        values = substitute(right, gaps, up, yends_ref[4], low, high, ny)
+        through = [ythrough_ref[j] for j in range(ny - 1)]
+        sums = [ysums_ref[j] for j in range(ny)]
+        values = substitute(sums, through, gaps, up, yends_ref[4], low, high, ny)
         for j in range(ny):
             out_ref[pl.ds(j, nx, stride=ny), :] = rows_y(p_ref, j) + values[j]
 
@@ -385,7 +404,7 @@
         updated_body,
         [(cells, nz)],
         [(far_y + 1, nx, nz), (NEAR_Y + 1, nx, nz)],
-        far_y_got, y_tree, yright, half, pressure, yup, yends,
+        far_y_got, y_tree, ysums, half, pressure, yup, ythrough, yends,
         name="updated",
     )
     return updated.reshape(nx, ny, nz)

time: 58.7 us -> 58.7 us (level)
  no operation moved by 1% of the time
where the time goes in v6:
time: 58.7 us; the launch traced here: 58.5 us
  blocking collectives  54 us (92%)
  Pallas kernels  2.49 us (4%)
  starting transfers between devices  1.92 us (3%)
    all_to_all x1, blocking collectives, local_step(): lax.all_to_all(far_x_send, 'gx', 0, 0, axis_index_groups=far_x_groups)  16.5 us
    all_to_all x1, blocking collectives, local_step(): near_x = lax.all_to_all(near_x, 'gx', 0, 0, axis_index_groups=near_x_groups)  14.5 us
    all_to_all x1, blocking collectives, local_step(): lax.all_to_all(far_y_send, 'gy', 0, 0, axis_index_groups=far_y_groups)  14.3 us
    all_gather x1, blocking collectives, local_step(): lax.all_gather(pair_send, 'gy', axis=0, axis_index_groups=near_y_groups)  5.52 us
    all_gather x1, blocking collectives, local_step(): lax.all_gather(near_send, 'gy', axis=0, axis_index_groups=chip_groups)  3.17 us
    ppermute x1, starting transfers between devices, local_step(): far_got = lax.ppermute(far_send, 'gy', far_pairs)  1.92 us
    pallas_call x6, Pallas kernels, call(): pl.pallas_call(body, out_shape=[jax.ShapeDtypeStruct(s, F32) for s in sha...  1.41 us
  transfers between devices with their start and end apart: 1, of which 0 were waited for; matrix products, arithmetic and copies ran while one was open for 0% of the time, Pallas kernels for 1%

profile of v6, /device:TPU:8, one launch (start us, length us, event | category | flops | bytes accessed | tf_op | source)
XLA Modules:
  0.0 58.5 jit_solution(7217644917217686380)
XLA Ops:
  0.0 1.1 %halves.1 = (f32[256,128]{1,0:T(8,128)S(1)}, f32[2,16,128]{2,1,0:T(8,128)S(1)}, f32[2,16,128]{2,1,0:T(8,128)S(1)}, f32[256,128]{1,0:T(8,128)S(1)}, f32[256,128]{1,0:T(8,128)S(1)}, /*index=5*/bf16[256,128]{1,0:T(8,128)(2,1)S(1)}) custom-call(f32[256,128]{1,0:T(8,128)} %bitcast.10, f32[256,128]{1,0:T(8,128)} %bitcast.11, bf16[256,128]{1,0:T(8,128)(2,1)} %bitcast.12, ...), custom_call_target="tpu_custom_call" | custom-call | tf_op jit(solution)/shard_map/halves/pallas_call | solution.py:196
  1.1 1.9 %collective-permute-start = (f32[2,16,128]{2,1,0:T(8,128)S(1)}, f32[2,16,128]{2,1,0:T(8,128)S(1)}, u32[]{:S(2)}, u32[]{:S(2)}) collective-permute-start(f32[2,16,128]{2,1,0:T(8,128)S(1)} %get-tuple-element.34), channel_id=1, source_target_pairs={{32,64},{64,32},{96,128},{128,96},{160,192},{192,160},{224,256},{2... | collective-permute-start | bytes 49160 | tf_op jit(solution)/shard_map/ppermute | solution.py:219
  3.0 0.3 inner.1
  3.3 3.2 %all-gather = f32[4,16,128]{2,1,0:T(8,128)S(1)} all-gather(f32[2,16,128]{2,1,0:T(8,128)S(1)} %get-tuple-element.35), channel_id=2, replica_groups={{0,32},{64,96},{128,160},{192,224},{256,288},{320,352},{384,416},{448,4..., dimensions={0}, use_global_device_ids=true | all-gather | bytes 49152 | tf_op jit(solution)/shard_map/all_gather | solution.py:220
  6.5 0.0 collective-permute-done.far_ref
  6.5 0.1 edges.1
  6.6 14.5 %all_to_all.15.got_ref = f32[8,5,16,128]{3,2,1,0:T(8,128)S(1)} all-to-all(f32[8,5,16,128]{3,2,1,0:T(8,128)S(1)} %get-tuple-element.39), channel_id=1, replica_groups={{0,1,2,3,4,5,6,7},{8,9,10,11,12,13,14,15},{16,17,18,19,20,21,22,23},{24..., dimensions={0} | all-to-all | bytes 655360 | tf_op jit(solution)/shard_map/all_to_all | solution.py:300
  21.1 16.5 %all_to_all.16.got_ref = f32[4,5,16,128]{3,2,1,0:T(8,128)S(1)} all-to-all(f32[4,5,16,128]{3,2,1,0:T(8,128)S(1)} %get-tuple-element.40), channel_id=1, replica_groups={{0,8,20,28},{1,9,21,29},{2,10,22,30},{3,11,23,31},{4,12,16,24},{5,13,17..., dimensions={0} | all-to-all | bytes 327680 | tf_op jit(solution)/shard_map/all_to_all | solution.py:314
  37.7 0.1 along_x.1
  37.8 5.5 %all-gather.1 = f32[20,16,128]{2,1,0:T(8,128)S(1)} all-gather(f32[5,16,128]{2,1,0:T(8,128)S(1)} %get-tuple-element.48), channel_id=3, replica_groups={{0,32,64,96},{128,160,192,224},{256,288,320,352},{384,416,448,480},{1,3..., dimensions={0}, use_global_device_ids=true | all-gather | bytes 204800 | tf_op jit(solution)/shard_map/all_gather | solution.py:360
  43.4 14.3 %all_to_all.17.got_ref = f32[4,5,16,128]{3,2,1,0:T(8,128)S(1)} all-to-all(f32[4,5,16,128]{3,2,1,0:T(8,128)S(1)} %get-tuple-element.49), channel_id=1, replica_groups={{0,128,320,448},{32,160,352,480},{64,192,256,384},{96,224,288,416},{1,1..., dimensions={0} | all-to-all | bytes 327680 | tf_op jit(solution)/shard_map/all_to_all | solution.py:374
  57.6 0.8 %updated.1 = f32[256,128]{1,0:T(8,128)} custom-call(f32[4,5,16,128]{3,2,1,0:T(8,128)S(1)} %all_to_all.17.got_ref, f32[9,16,128]{2,1,0:T(8,128)S(1)} %get-tuple-element.50.tree_ref, f32[16,16,128]{2,1,0:T(8,128)S(1)} %get-tuple-element.51.ysums_ref, f32[256,128]{1,0:T(8,128)S(1)} %get-tuple-element.32.half_ref, f32[256,128]{1,0:T(8,128)S(1)} %get-tuple-element.29.p_ref, ...), custom_call_target="tpu_custom_call" | custom-call | tf_op jit(solution)/shard_map/updated/pallas_call | solution.py:155
  (2 shorter events, 0.1 us)
Async XLA Ops:
  1.1 5.4 %collective-permute-start = (f32[2,16,128]{2,1,0:T(8,128)S(1)}, f32[2,16,128]{2,1,0:T(8,128)S(1)}, u32[]{:S(2)}, u32[]{:S(2)}) collective-permute-start(f32[2,16,128]{2,1,0:T(8,128)S(1)} %get-tuple-element.34), channel_id=1, source_target_pairs={{32,64},{64,32},{96,128},{128,96},{160,192},{192,160},{224,256},{2... | collective-permute-start | bytes 49160 | tf_op jit(solution)/shard_map/ppermute | solution.py:219

commit v7 on v6

--- a/solution.py
+++ b/solution.py
@@ -13,6 +13,9 @@
 NEAR_Y = 2 * CORES
 PICKS = ((0, 0, 1, 1), (1, 1, 0, 0))
 F32 = jnp.float32
+NEAR_X_ORDER = (7, 6, 5, 4, 3, 2, 1, 0)
+FAR_X_ORDER = (3, 2, 1, 0)
+FAR_Y_ORDER = (2, 3, 1, 0)
 
 
 def join(left, right):
@@ -297,10 +300,10 @@
         edges_body, [(nx, ny, nz), (NEAR_X, 5, ny, nz)], [(cells, nz)],
         right0, pressure, half, far_got, near_got, xup, xdown, xends, name="edges",
     )
-    near_x = lax.all_to_all(near_x, "gx", 0, 0, axis_index_groups=near_x_groups)
+    near_x = lax.all_to_all(near_x, "gx", 0, 0, axis_index_groups=[[g[i] for i in NEAR_X_ORDER] for g in near_x_groups])
 
     def ring_body(got_ref, send_ref, tree_ref):
-        pieces = [tuple(got_ref[n, k] for k in range(5)) for n in range(NEAR_X)]
+        pieces = [tuple(got_ref[NEAR_X_ORDER.index(n), k] for k in range(5)) for n in range(NEAR_X)]
         merged, tree = join_all(pieces)
         for k in range(5):
             for target in range(far_x):
@@ -311,7 +314,7 @@
     far_x_send, x_tree = call(
         ring_body, [(far_x, 5, ny, nz), (3 * (NEAR_X - 1), ny, nz)], [], near_x, name="x_ring"
     )
-    far_x_got = lax.all_to_all(far_x_send, "gx", 0, 0, axis_index_groups=far_x_groups)
+    far_x_got = lax.all_to_all(far_x_send, "gx", 0, 0, axis_index_groups=[[g[i] for i in FAR_X_ORDER] for g in far_x_groups])
 
     def along_x_body(
         got_ref, tree_ref, xsums_ref, half_ref, ratio_ref, p_ref, xup_ref, xthrough_ref, xends_ref,
@@ -321,7 +324,7 @@
         place = lax.axis_index("gx")
         far = place // NEAR_X
         near = lax.rem(place, NEAR_X)
-        pieces = [tuple(got_ref[n, k] for k in range(5)) for n in range(far_x)]
+        pieces = [tuple(got_ref[FAR_X_ORDER.index(n), k] for k in range(5)) for n in range(far_x)]
         _, tree = join_all(pieces)
         fluxes = face_fluxes(tree, None, None)
         zero = jnp.zeros((ny, nz), F32)
@@ -371,7 +374,7 @@
     far_y_send, y_tree = call(
         pair_body, [(far_y, 5, nx, nz), (3 * (NEAR_Y - 1), nx, nz)], [], pair_got, name="y_pair"
     )
-    far_y_got = lax.all_to_all(far_y_send, "gy", 0, 0, axis_index_groups=far_y_groups)
+    far_y_got = lax.all_to_all(far_y_send, "gy", 0, 0, axis_index_groups=[[g[i] for i in FAR_Y_ORDER] for g in far_y_groups])
 
     def updated_body(
         got_ref, tree_ref, ysums_ref, half_ref, p_ref, yup_ref, ythrough_ref, yends_ref, out_ref, far_faces, near_faces
@@ -379,7 +382,7 @@
         place = lax.axis_index("gy")
         far = place // NEAR_Y
         near = lax.rem(place, NEAR_Y)
-        pieces = [tuple(got_ref[n, k] for k in range(5)) for n in range(far_y)]
+        pieces = [tuple(got_ref[FAR_Y_ORDER.index(n), k] for k in range(5)) for n in range(far_y)]
         _, tree = join_all(pieces)
         zero = jnp.zeros((nx, nz), F32)
         for k, value in enumerate(face_fluxes(tree, None, None)):

time: 58.7 us -> 56.2 us (0.957)
  the two profiles are of different devices: /device:TPU:8 before, /device:TPU:1 now
where the time goes in v7:
time: 56.2 us; the launch traced here: 56 us
  blocking collectives  48.8 us (87%)
  starting transfers between devices  4.59 us (8%)
  Pallas kernels  2.49 us (4%)
    all_to_all x1, blocking collectives, local_step(): lax.all_to_all(far_x_send, 'gx', 0, 0, axis_index_groups=[[g[i] for i in...  13.1 us
    all_to_all x1, blocking collectives, local_step(): lax.all_to_all(far_y_send, 'gy', 0, 0, axis_index_groups=[[g[i] for i in...  12.5 us
    all_to_all x1, blocking collectives, local_step(): lax.all_to_all(near_x, 'gx', 0, 0, axis_index_groups=[[g[i] for i in NEAR...  10.2 us
    all_gather x1, blocking collectives, local_step(): lax.all_gather(pair_send, 'gy', axis=0, axis_index_groups=near_y_groups)  8.54 us
    ppermute x1, starting transfers between devices, local_step(): far_got = lax.ppermute(far_send, 'gy', far_pairs)  4.59 us
    all_gather x1, blocking collectives, local_step(): lax.all_gather(near_send, 'gy', axis=0, axis_index_groups=chip_groups)  4.44 us
    pallas_call x6, Pallas kernels, call(): pl.pallas_call(body, out_shape=[jax.ShapeDtypeStruct(s, F32) for s in sha...  1.41 us
  transfers between devices with their start and end apart: 1, of which 0 were waited for; matrix products, arithmetic and copies ran while one was open for 0% of the time, Pallas kernels for 1%

profile of v7, /device:TPU:1, one launch (start us, length us, event | category | flops | bytes accessed | tf_op | source)
XLA Modules:
  0.0 56.0 jit_solution(9798825931989281654)
XLA Ops:
  0.0 1.1 %halves.1 = (f32[256,128]{1,0:T(8,128)S(1)}, f32[2,16,128]{2,1,0:T(8,128)S(1)}, f32[2,16,128]{2,1,0:T(8,128)S(1)}, f32[256,128]{1,0:T(8,128)S(1)}, f32[256,128]{1,0:T(8,128)S(1)}, /*index=5*/bf16[256,128]{1,0:T(8,128)(2,1)S(1)}) custom-call(f32[256,128]{1,0:T(8,128)} %bitcast.10, f32[256,128]{1,0:T(8,128)} %bitcast.11, bf16[256,128]{1,0:T(8,128)(2,1)} %bitcast.12, ...), custom_call_target="tpu_custom_call" | custom-call | tf_op jit(solution)/shard_map/halves/pallas_call | solution.py:199
  1.1 4.6 %collective-permute-start = (f32[2,16,128]{2,1,0:T(8,128)S(1)}, f32[2,16,128]{2,1,0:T(8,128)S(1)}, u32[]{:S(2)}, u32[]{:S(2)}) collective-permute-start(f32[2,16,128]{2,1,0:T(8,128)S(1)} %get-tuple-element.34), channel_id=1, source_target_pairs={{32,64},{64,32},{96,128},{128,96},{160,192},{192,160},{224,256},{2... | collective-permute-start | bytes 49160 | tf_op jit(solution)/shard_map/ppermute | solution.py:222
  5.7 0.3 inner.1
  6.0 4.4 %all-gather = f32[4,16,128]{2,1,0:T(8,128)S(1)} all-gather(f32[2,16,128]{2,1,0:T(8,128)S(1)} %get-tuple-element.35), channel_id=2, replica_groups={{0,32},{64,96},{128,160},{192,224},{256,288},{320,352},{384,416},{448,4..., dimensions={0}, use_global_device_ids=true | all-gather | bytes 49152 | tf_op jit(solution)/shard_map/all_gather | solution.py:223
  10.4 0.0 collective-permute-done.far_ref
  10.4 0.1 edges.1
  10.5 10.2 %all_to_all.15.got_ref = f32[8,5,16,128]{3,2,1,0:T(8,128)S(1)} all-to-all(f32[8,5,16,128]{3,2,1,0:T(8,128)S(1)} %get-tuple-element.39), channel_id=1, replica_groups={{7,6,5,4,3,2,1,0},{15,14,13,12,11,10,9,8},{23,22,21,20,19,18,17,16},{31..., dimensions={0} | all-to-all | bytes 655360 | tf_op jit(solution)/shard_map/all_to_all | solution.py:303
  20.8 13.1 %all_to_all.16.got_ref = f32[4,5,16,128]{3,2,1,0:T(8,128)S(1)} all-to-all(f32[4,5,16,128]{3,2,1,0:T(8,128)S(1)} %get-tuple-element.40), channel_id=1, replica_groups={{28,20,8,0},{29,21,9,1},{30,22,10,2},{31,23,11,3},{24,16,12,4},{25,17,1..., dimensions={0} | all-to-all | bytes 327680 | tf_op jit(solution)/shard_map/all_to_all | solution.py:317
  33.9 0.1 along_x.1
  34.0 8.5 %all-gather.1 = f32[20,16,128]{2,1,0:T(8,128)S(1)} all-gather(f32[5,16,128]{2,1,0:T(8,128)S(1)} %get-tuple-element.48), channel_id=3, replica_groups={{0,32,64,96},{128,160,192,224},{256,288,320,352},{384,416,448,480},{1,3..., dimensions={0}, use_global_device_ids=true | all-gather | bytes 204800 | tf_op jit(solution)/shard_map/all_gather | solution.py:363
  42.6 12.5 %all_to_all.17.got_ref = f32[4,5,16,128]{3,2,1,0:T(8,128)S(1)} all-to-all(f32[4,5,16,128]{3,2,1,0:T(8,128)S(1)} %get-tuple-element.49), channel_id=1, replica_groups={{320,448,128,0},{352,480,160,32},{256,384,192,64},{288,416,224,96},{321..., dimensions={0} | all-to-all | bytes 327680 | tf_op jit(solution)/shard_map/all_to_all | solution.py:377
  55.1 0.8 %updated.1 = f32[256,128]{1,0:T(8,128)} custom-call(f32[4,5,16,128]{3,2,1,0:T(8,128)S(1)} %all_to_all.17.got_ref, f32[9,16,128]{2,1,0:T(8,128)S(1)} %get-tuple-element.50.tree_ref, f32[16,16,128]{2,1,0:T(8,128)S(1)} %get-tuple-element.51.ysums_ref, f32[256,128]{1,0:T(8,128)S(1)} %get-tuple-element.32.half_ref, f32[256,128]{1,0:T(8,128)S(1)} %get-tuple-element.29.p_ref, ...), custom_call_target="tpu_custom_call" | custom-call | tf_op jit(solution)/shard_map/updated/pallas_call | solution.py:158
  (2 shorter events, 0.1 us)
Async XLA Ops:
  1.1 9.3 %collective-permute-start = (f32[2,16,128]{2,1,0:T(8,128)S(1)}, f32[2,16,128]{2,1,0:T(8,128)S(1)}, u32[]{:S(2)}, u32[]{:S(2)}) collective-permute-start(f32[2,16,128]{2,1,0:T(8,128)S(1)} %get-tuple-element.34), channel_id=1, source_target_pairs={{32,64},{64,32},{96,128},{128,96},{160,192},{192,160},{224,256},{2... | collective-permute-start | bytes 49160 | tf_op jit(solution)/shard_map/ppermute | solution.py:222

commit v8 on v7

--- a/solution.py
+++ b/solution.py
@@ -11,10 +11,10 @@
 CORES = 2
 NEAR_X = 2 * RING_X
 NEAR_Y = 2 * CORES
-PICKS = ((0, 0, 1, 1), (1, 1, 0, 0))
+PICKS = ((0, 1, 1, 0), (1, 0, 0, 1))
 F32 = jnp.float32
 NEAR_X_ORDER = (7, 6, 5, 4, 3, 2, 1, 0)
-FAR_X_ORDER = (3, 2, 1, 0)
+FAR_X_ORDER = (2, 3, 1, 0)
 FAR_Y_ORDER = (2, 3, 1, 0)
 
 

time: 56.2 us -> 54.6 us (0.972)
  blocking collectives: 48.8 us -> 47.2 us
    all_gather x1, blocking collectives: 8.54 us -> 7.24 us  [local_step(): lax.all_gather(pair_send, 'gy', axis=0, axis_index_groups=near_y_groups)]
    all_to_all x1, blocking collectives: 12.5 us -> 11.8 us  [local_step(): lax.all_to_all(far_y_send, 'gy', 0, 0, axis_index_groups=[[g[i] for i in...]
where the time goes in v8:
time: 54.6 us; the launch traced here: 54.3 us
  blocking collectives  47.2 us (86%)
  starting transfers between devices  4.59 us (8%)
  Pallas kernels  2.49 us (5%)
    all_to_all x1, blocking collectives, local_step(): lax.all_to_all(far_x_send, 'gx', 0, 0, axis_index_groups=[[g[i] for i in...  13.5 us
    all_to_all x1, blocking collectives, local_step(): lax.all_to_all(far_y_send, 'gy', 0, 0, axis_index_groups=[[g[i] for i in...  11.8 us
    all_to_all x1, blocking collectives, local_step(): lax.all_to_all(near_x, 'gx', 0, 0, axis_index_groups=[[g[i] for i in NEAR...  10.2 us
    all_gather x1, blocking collectives, local_step(): lax.all_gather(pair_send, 'gy', axis=0, axis_index_groups=near_y_groups)  7.24 us
    ppermute x1, starting transfers between devices, local_step(): far_got = lax.ppermute(far_send, 'gy', far_pairs)  4.59 us
    all_gather x1, blocking collectives, local_step(): lax.all_gather(near_send, 'gy', axis=0, axis_index_groups=chip_groups)  4.44 us
    pallas_call x6, Pallas kernels, call(): pl.pallas_call(body, out_shape=[jax.ShapeDtypeStruct(s, F32) for s in sha...  1.41 us
  transfers between devices with their start and end apart: 1, of which 0 were waited for; matrix products, arithmetic and copies ran while one was open for 0% of the time, Pallas kernels for 1%

profile of v8, /device:TPU:1, one launch (start us, length us, event | category | flops | bytes accessed | tf_op | source)
XLA Modules:
  0.0 54.3 jit_solution(6675023343285762970)
XLA Ops:
  0.0 1.1 %halves.1 = (f32[256,128]{1,0:T(8,128)S(1)}, f32[2,16,128]{2,1,0:T(8,128)S(1)}, f32[2,16,128]{2,1,0:T(8,128)S(1)}, f32[256,128]{1,0:T(8,128)S(1)}, f32[256,128]{1,0:T(8,128)S(1)}, /*index=5*/bf16[256,128]{1,0:T(8,128)(2,1)S(1)}) custom-call(f32[256,128]{1,0:T(8,128)} %bitcast.10, f32[256,128]{1,0:T(8,128)} %bitcast.11, bf16[256,128]{1,0:T(8,128)(2,1)} %bitcast.12, ...), custom_call_target="tpu_custom_call" | custom-call | tf_op jit(solution)/shard_map/halves/pallas_call | solution.py:199
  1.1 4.6 %collective-permute-start = (f32[2,16,128]{2,1,0:T(8,128)S(1)}, f32[2,16,128]{2,1,0:T(8,128)S(1)}, u32[]{:S(2)}, u32[]{:S(2)}) collective-permute-start(f32[2,16,128]{2,1,0:T(8,128)S(1)} %get-tuple-element.34), channel_id=1, source_target_pairs={{32,64},{64,32},{96,128},{128,96},{160,192},{192,160},{224,256},{2... | collective-permute-start | bytes 49160 | tf_op jit(solution)/shard_map/ppermute | solution.py:222
  5.7 0.3 inner.1
  6.0 4.4 %all-gather = f32[4,16,128]{2,1,0:T(8,128)S(1)} all-gather(f32[2,16,128]{2,1,0:T(8,128)S(1)} %get-tuple-element.35), channel_id=2, replica_groups={{0,32},{64,96},{128,160},{192,224},{256,288},{320,352},{384,416},{448,4..., dimensions={0}, use_global_device_ids=true | all-gather | bytes 49152 | tf_op jit(solution)/shard_map/all_gather | solution.py:223
  10.4 0.0 collective-permute-done.far_ref
  10.4 0.1 edges.1
  10.5 10.2 %all_to_all.15.got_ref = f32[8,5,16,128]{3,2,1,0:T(8,128)S(1)} all-to-all(f32[8,5,16,128]{3,2,1,0:T(8,128)S(1)} %get-tuple-element.39), channel_id=1, replica_groups={{7,6,5,4,3,2,1,0},{15,14,13,12,11,10,9,8},{23,22,21,20,19,18,17,16},{31..., dimensions={0} | all-to-all | bytes 655360 | tf_op jit(solution)/shard_map/all_to_all | solution.py:303
  20.8 13.5 %all_to_all.16.got_ref = f32[4,5,16,128]{3,2,1,0:T(8,128)S(1)} all-to-all(f32[4,5,16,128]{3,2,1,0:T(8,128)S(1)} %get-tuple-element.40), channel_id=1, replica_groups={{20,24,12,0},{21,25,13,1},{22,26,14,2},{23,27,15,3},{16,28,8,4},{17,29,..., dimensions={0} | all-to-all | bytes 327680 | tf_op jit(solution)/shard_map/all_to_all | solution.py:317
  34.3 0.1 along_x.1
  34.4 7.2 %all-gather.1 = f32[20,16,128]{2,1,0:T(8,128)S(1)} all-gather(f32[5,16,128]{2,1,0:T(8,128)S(1)} %get-tuple-element.48), channel_id=3, replica_groups={{0,32,64,96},{128,160,192,224},{256,288,320,352},{384,416,448,480},{1,3..., dimensions={0}, use_global_device_ids=true | all-gather | bytes 204800 | tf_op jit(solution)/shard_map/all_gather | solution.py:363
  41.7 11.8 %all_to_all.17.got_ref = f32[4,5,16,128]{3,2,1,0:T(8,128)S(1)} all-to-all(f32[4,5,16,128]{3,2,1,0:T(8,128)S(1)} %get-tuple-element.49), channel_id=1, replica_groups={{320,384,192,0},{352,416,224,32},{256,448,128,64},{288,480,160,96},{321..., dimensions={0} | all-to-all | bytes 327680 | tf_op jit(solution)/shard_map/all_to_all | solution.py:377
  53.5 0.8 %updated.1 = f32[256,128]{1,0:T(8,128)} custom-call(f32[4,5,16,128]{3,2,1,0:T(8,128)S(1)} %all_to_all.17.got_ref, f32[9,16,128]{2,1,0:T(8,128)S(1)} %get-tuple-element.50.tree_ref, f32[16,16,128]{2,1,0:T(8,128)S(1)} %get-tuple-element.51.ysums_ref, f32[256,128]{1,0:T(8,128)S(1)} %get-tuple-element.32.half_ref, f32[256,128]{1,0:T(8,128)S(1)} %get-tuple-element.29.p_ref, ...), custom_call_target="tpu_custom_call" | custom-call | tf_op jit(solution)/shard_map/updated/pallas_call | solution.py:158
  (2 shorter events, 0.1 us)
Async XLA Ops:
  1.1 9.3 %collective-permute-start = (f32[2,16,128]{2,1,0:T(8,128)S(1)}, f32[2,16,128]{2,1,0:T(8,128)S(1)}, u32[]{:S(2)}, u32[]{:S(2)}) collective-permute-start(f32[2,16,128]{2,1,0:T(8,128)S(1)} %get-tuple-element.34), channel_id=1, source_target_pairs={{32,64},{64,32},{96,128},{128,96},{160,192},{192,160},{224,256},{2... | collective-permute-start | bytes 49160 | tf_op jit(solution)/shard_map/ppermute | solution.py:222

commit v9 on v8

--- a/solution.py
+++ b/solution.py
@@ -13,7 +13,7 @@
 NEAR_Y = 2 * CORES
 PICKS = ((0, 1, 1, 0), (1, 0, 0, 1))
 F32 = jnp.float32
-NEAR_X_ORDER = (7, 6, 5, 4, 3, 2, 1, 0)
+NEAR_X_ORDER = (6, 7, 5, 4, 3, 2, 1, 0)
 FAR_X_ORDER = (2, 3, 1, 0)
 FAR_Y_ORDER = (2, 3, 1, 0)
 

time: 54.6 us -> 54.1 us (level)
  blocking collectives: 47.2 us -> 46.3 us
    all_gather x1, blocking collectives: 7.24 us -> 8.41 us  [local_step(): lax.all_gather(pair_send, 'gy', axis=0, axis_index_groups=near_y_groups)]
    all_to_all x1, blocking collectives: 10.2 us -> 9.09 us  [local_step(): lax.all_to_all(near_x, 'gx', 0, 0, axis_index_groups=[[g[i] for i in NEAR...]
    all_to_all x1, blocking collectives: 13.5 us -> 12.9 us  [local_step(): lax.all_to_all(far_x_send, 'gx', 0, 0, axis_index_groups=[[g[i] for i in...]
where the time goes in v9:
time: 54.1 us; the launch traced here: 53.4 us
  blocking collectives  46.3 us (86%)
  starting transfers between devices  4.59 us (8%)
  Pallas kernels  2.49 us (5%)
    all_to_all x1, blocking collectives, local_step(): lax.all_to_all(far_x_send, 'gx', 0, 0, axis_index_groups=[[g[i] for i in...  12.9 us
    all_to_all x1, blocking collectives, local_step(): lax.all_to_all(far_y_send, 'gy', 0, 0, axis_index_groups=[[g[i] for i in...  11.5 us
    all_to_all x1, blocking collectives, local_step(): lax.all_to_all(near_x, 'gx', 0, 0, axis_index_groups=[[g[i] for i in NEAR...  9.09 us
    all_gather x1, blocking collectives, local_step(): lax.all_gather(pair_send, 'gy', axis=0, axis_index_groups=near_y_groups)  8.41 us
    ppermute x1, starting transfers between devices, local_step(): far_got = lax.ppermute(far_send, 'gy', far_pairs)  4.59 us
    all_gather x1, blocking collectives, local_step(): lax.all_gather(near_send, 'gy', axis=0, axis_index_groups=chip_groups)  4.44 us
    pallas_call x6, Pallas kernels, call(): pl.pallas_call(body, out_shape=[jax.ShapeDtypeStruct(s, F32) for s in sha...  1.41 us
    pallas_call x1, Pallas kernels, local_step(): pl.pallas_call(halves_body, out_shape=[jax.ShapeDtypeStruct((cells, nz),...  1.08 us
  transfers between devices with their start and end apart: 1, of which 0 were waited for; matrix products, arithmetic and copies ran while one was open for 0% of the time, Pallas kernels for 1%

profile of v9, /device:TPU:1, one launch (start us, length us, event | category | flops | bytes accessed | tf_op | source)
XLA Modules:
  0.0 53.4 jit_solution(17414883363725890638)
XLA Ops:
  0.0 1.1 %halves.1 = (f32[256,128]{1,0:T(8,128)S(1)}, f32[2,16,128]{2,1,0:T(8,128)S(1)}, f32[2,16,128]{2,1,0:T(8,128)S(1)}, f32[256,128]{1,0:T(8,128)S(1)}, f32[256,128]{1,0:T(8,128)S(1)}, /*index=5*/bf16[256,128]{1,0:T(8,128)(2,1)S(1)}) custom-call(f32[256,128]{1,0:T(8,128)} %bitcast.10, f32[256,128]{1,0:T(8,128)} %bitcast.11, bf16[256,128]{1,0:T(8,128)(2,1)} %bitcast.12, ...), custom_call_target="tpu_custom_call" | custom-call | tf_op jit(solution)/shard_map/halves/pallas_call | solution.py:199
  1.1 4.6 %collective-permute-start = (f32[2,16,128]{2,1,0:T(8,128)S(1)}, f32[2,16,128]{2,1,0:T(8,128)S(1)}, u32[]{:S(2)}, u32[]{:S(2)}) collective-permute-start(f32[2,16,128]{2,1,0:T(8,128)S(1)} %get-tuple-element.34), channel_id=1, source_target_pairs={{32,64},{64,32},{96,128},{128,96},{160,192},{192,160},{224,256},{2... | collective-permute-start | bytes 49160 | tf_op jit(solution)/shard_map/ppermute | solution.py:222
  5.7 0.3 inner.1
  6.0 4.4 %all-gather = f32[4,16,128]{2,1,0:T(8,128)S(1)} all-gather(f32[2,16,128]{2,1,0:T(8,128)S(1)} %get-tuple-element.35), channel_id=2, replica_groups={{0,32},{64,96},{128,160},{192,224},{256,288},{320,352},{384,416},{448,4..., dimensions={0}, use_global_device_ids=true | all-gather | bytes 49152 | tf_op jit(solution)/shard_map/all_gather | solution.py:223
  10.4 0.0 collective-permute-done.far_ref
  10.4 0.1 edges.1
  10.5 9.1 %all_to_all.15.got_ref = f32[8,5,16,128]{3,2,1,0:T(8,128)S(1)} all-to-all(f32[8,5,16,128]{3,2,1,0:T(8,128)S(1)} %get-tuple-element.39), channel_id=1, replica_groups={{6,7,5,4,3,2,1,0},{14,15,13,12,11,10,9,8},{22,23,21,20,19,18,17,16},{30..., dimensions={0} | all-to-all | bytes 655360 | tf_op jit(solution)/shard_map/all_to_all | solution.py:303
  19.7 12.9 %all_to_all.16.got_ref = f32[4,5,16,128]{3,2,1,0:T(8,128)S(1)} all-to-all(f32[4,5,16,128]{3,2,1,0:T(8,128)S(1)} %get-tuple-element.40), channel_id=1, replica_groups={{20,24,12,0},{21,25,13,1},{22,26,14,2},{23,27,15,3},{16,28,8,4},{17,29,..., dimensions={0} | all-to-all | bytes 327680 | tf_op jit(solution)/shard_map/all_to_all | solution.py:317
  32.5 0.1 along_x.1
  32.7 8.4 %all-gather.1 = f32[20,16,128]{2,1,0:T(8,128)S(1)} all-gather(f32[5,16,128]{2,1,0:T(8,128)S(1)} %get-tuple-element.48), channel_id=3, replica_groups={{0,32,64,96},{128,160,192,224},{256,288,320,352},{384,416,448,480},{1,3..., dimensions={0}, use_global_device_ids=true | all-gather | bytes 204800 | tf_op jit(solution)/shard_map/all_gather | solution.py:363
  41.1 11.5 %all_to_all.17.got_ref = f32[4,5,16,128]{3,2,1,0:T(8,128)S(1)} all-to-all(f32[4,5,16,128]{3,2,1,0:T(8,128)S(1)} %get-tuple-element.49), channel_id=1, replica_groups={{320,384,192,0},{352,416,224,32},{256,448,128,64},{288,480,160,96},{321..., dimensions={0} | all-to-all | bytes 327680 | tf_op jit(solution)/shard_map/all_to_all | solution.py:377
  52.6 0.8 %updated.1 = f32[256,128]{1,0:T(8,128)} custom-call(f32[4,5,16,128]{3,2,1,0:T(8,128)S(1)} %all_to_all.17.got_ref, f32[9,16,128]{2,1,0:T(8,128)S(1)} %get-tuple-element.50.tree_ref, f32[16,16,128]{2,1,0:T(8,128)S(1)} %get-tuple-element.51.ysums_ref, f32[256,128]{1,0:T(8,128)S(1)} %get-tuple-element.32.half_ref, f32[256,128]{1,0:T(8,128)S(1)} %get-tuple-element.29.p_ref, ...), custom_call_target="tpu_custom_call" | custom-call | tf_op jit(solution)/shard_map/updated/pallas_call | solution.py:158
  (2 shorter events, 0.1 us)
Async XLA Ops:
  1.1 9.3 %collective-permute-start = (f32[2,16,128]{2,1,0:T(8,128)S(1)}, f32[2,16,128]{2,1,0:T(8,128)S(1)}, u32[]{:S(2)}, u32[]{:S(2)}) collective-permute-start(f32[2,16,128]{2,1,0:T(8,128)S(1)} %get-tuple-element.34), channel_id=1, source_target_pairs={{32,64},{64,32},{96,128},{128,96},{160,192},{192,160},{224,256},{2... | collective-permute-start | bytes 49160 | tf_op jit(solution)/shard_map/ppermute | solution.py:222

commit v10 on v9

--- a/solution.py
+++ b/solution.py
@@ -15,7 +15,7 @@
 F32 = jnp.float32
 NEAR_X_ORDER = (6, 7, 5, 4, 3, 2, 1, 0)
 FAR_X_ORDER = (2, 3, 1, 0)
-FAR_Y_ORDER = (2, 3, 1, 0)
+FAR_Y_ORDER = (2, 1, 3, 0)
 
 
 def join(left, right):

time: 54.1 us -> 54.1 us (level)
  no operation moved by 1% of the time
where the time goes in v10:
time: 54.1 us; the launch traced here: 53.5 us
  blocking collectives  46.4 us (86%)
  starting transfers between devices  4.59 us (8%)
  Pallas kernels  2.49 us (5%)
    all_to_all x1, blocking collectives, local_step(): lax.all_to_all(far_x_send, 'gx', 0, 0, axis_index_groups=[[g[i] for i in...  12.9 us
    all_to_all x1, blocking collectives, local_step(): lax.all_to_all(far_y_send, 'gy', 0, 0, axis_index_groups=[[g[i] for i in...  11.6 us
    all_to_all x1, blocking collectives, local_step(): lax.all_to_all(near_x, 'gx', 0, 0, axis_index_groups=[[g[i] for i in NEAR...  9.09 us
    all_gather x1, blocking collectives, local_step(): lax.all_gather(pair_send, 'gy', axis=0, axis_index_groups=near_y_groups)  8.41 us
    ppermute x1, starting transfers between devices, local_step(): far_got = lax.ppermute(far_send, 'gy', far_pairs)  4.59 us
    all_gather x1, blocking collectives, local_step(): lax.all_gather(near_send, 'gy', axis=0, axis_index_groups=chip_groups)  4.44 us
    pallas_call x6, Pallas kernels, call(): pl.pallas_call(body, out_shape=[jax.ShapeDtypeStruct(s, F32) for s in sha...  1.41 us
    pallas_call x1, Pallas kernels, local_step(): pl.pallas_call(halves_body, out_shape=[jax.ShapeDtypeStruct((cells, nz),...  1.08 us
  transfers between devices with their start and end apart: 1, of which 0 were waited for; matrix products, arithmetic and copies ran while one was open for 0% of the time, Pallas kernels for 1%

profile of v10, /device:TPU:1, one launch (start us, length us, event | category | flops | bytes accessed | tf_op | source)
XLA Modules:
  0.0 53.5 jit_solution(12131789731566855734)
XLA Ops:
  0.0 1.1 %halves.1 = (f32[256,128]{1,0:T(8,128)S(1)}, f32[2,16,128]{2,1,0:T(8,128)S(1)}, f32[2,16,128]{2,1,0:T(8,128)S(1)}, f32[256,128]{1,0:T(8,128)S(1)}, f32[256,128]{1,0:T(8,128)S(1)}, /*index=5*/bf16[256,128]{1,0:T(8,128)(2,1)S(1)}) custom-call(f32[256,128]{1,0:T(8,128)} %bitcast.10, f32[256,128]{1,0:T(8,128)} %bitcast.11, bf16[256,128]{1,0:T(8,128)(2,1)} %bitcast.12, ...), custom_call_target="tpu_custom_call" | custom-call | tf_op jit(solution)/shard_map/halves/pallas_call | solution.py:199
  1.1 4.6 %collective-permute-start = (f32[2,16,128]{2,1,0:T(8,128)S(1)}, f32[2,16,128]{2,1,0:T(8,128)S(1)}, u32[]{:S(2)}, u32[]{:S(2)}) collective-permute-start(f32[2,16,128]{2,1,0:T(8,128)S(1)} %get-tuple-element.34), channel_id=1, source_target_pairs={{32,64},{64,32},{96,128},{128,96},{160,192},{192,160},{224,256},{2... | collective-permute-start | bytes 49160 | tf_op jit(solution)/shard_map/ppermute | solution.py:222
  5.7 0.3 inner.1
  6.0 4.4 %all-gather = f32[4,16,128]{2,1,0:T(8,128)S(1)} all-gather(f32[2,16,128]{2,1,0:T(8,128)S(1)} %get-tuple-element.35), channel_id=2, replica_groups={{0,32},{64,96},{128,160},{192,224},{256,288},{320,352},{384,416},{448,4..., dimensions={0}, use_global_device_ids=true | all-gather | bytes 49152 | tf_op jit(solution)/shard_map/all_gather | solution.py:223
  10.4 0.0 collective-permute-done.far_ref
  10.4 0.1 edges.1
  10.5 9.1 %all_to_all.15.got_ref = f32[8,5,16,128]{3,2,1,0:T(8,128)S(1)} all-to-all(f32[8,5,16,128]{3,2,1,0:T(8,128)S(1)} %get-tuple-element.39), channel_id=1, replica_groups={{6,7,5,4,3,2,1,0},{14,15,13,12,11,10,9,8},{22,23,21,20,19,18,17,16},{30..., dimensions={0} | all-to-all | bytes 655360 | tf_op jit(solution)/shard_map/all_to_all | solution.py:303
  19.7 12.9 %all_to_all.16.got_ref = f32[4,5,16,128]{3,2,1,0:T(8,128)S(1)} all-to-all(f32[4,5,16,128]{3,2,1,0:T(8,128)S(1)} %get-tuple-element.40), channel_id=1, replica_groups={{20,24,12,0},{21,25,13,1},{22,26,14,2},{23,27,15,3},{16,28,8,4},{17,29,..., dimensions={0} | all-to-all | bytes 327680 | tf_op jit(solution)/shard_map/all_to_all | solution.py:317
  32.5 0.1 along_x.1
  32.7 8.4 %all-gather.1 = f32[20,16,128]{2,1,0:T(8,128)S(1)} all-gather(f32[5,16,128]{2,1,0:T(8,128)S(1)} %get-tuple-element.48), channel_id=3, replica_groups={{0,32,64,96},{128,160,192,224},{256,288,320,352},{384,416,448,480},{1,3..., dimensions={0}, use_global_device_ids=true | all-gather | bytes 204800 | tf_op jit(solution)/shard_map/all_gather | solution.py:363
  41.1 11.6 %all_to_all.17.got_ref = f32[4,5,16,128]{3,2,1,0:T(8,128)S(1)} all-to-all(f32[4,5,16,128]{3,2,1,0:T(8,128)S(1)} %get-tuple-element.49), channel_id=1, replica_groups={{320,192,384,0},{352,224,416,32},{256,128,448,64},{288,160,480,96},{321..., dimensions={0} | all-to-all | bytes 327680 | tf_op jit(solution)/shard_map/all_to_all | solution.py:377
  52.7 0.8 %updated.1 = f32[256,128]{1,0:T(8,128)} custom-call(f32[4,5,16,128]{3,2,1,0:T(8,128)S(1)} %all_to_all.17.got_ref, f32[9,16,128]{2,1,0:T(8,128)S(1)} %get-tuple-element.50.tree_ref, f32[16,16,128]{2,1,0:T(8,128)S(1)} %get-tuple-element.51.ysums_ref, f32[256,128]{1,0:T(8,128)S(1)} %get-tuple-element.32.half_ref, f32[256,128]{1,0:T(8,128)S(1)} %get-tuple-element.29.p_ref, ...), custom_call_target="tpu_custom_call" | custom-call | tf_op jit(solution)/shard_map/updated/pallas_call | solution.py:158
  (2 shorter events, 0.1 us)
Async XLA Ops:
  1.1 9.3 %collective-permute-start = (f32[2,16,128]{2,1,0:T(8,128)S(1)}, f32[2,16,128]{2,1,0:T(8,128)S(1)}, u32[]{:S(2)}, u32[]{:S(2)}) collective-permute-start(f32[2,16,128]{2,1,0:T(8,128)S(1)} %get-tuple-element.34), channel_id=1, source_target_pairs={{32,64},{64,32},{96,128},{128,96},{160,192},{192,160},{224,256},{2... | collective-permute-start | bytes 49160 | tf_op jit(solution)/shard_map/ppermute | solution.py:222
